TPU v7x, 32 devices: a whole 2x2x4 slice. The times are simulated.
32 devices in a mesh: group: 4 (over y, core), member: 8 (over z, x).
Axes of the slice: x: 2, y: 2, z: 4, core: 2. Of those that a mesh axis runs over, the one named last changes fastest.
Arguments:
- fine_blocks: float32 [512, 5, 128, 128], P(('group', 'member')), may hold values from -6 to 6
- neighbours: int32 [512, 5], P(('group', 'member')), may hold values from 0 to 511, as said below
- slot_one: int32 [512, 5], P(('group', 'member')), may hold values from 0 to 4
- pair_one: int32 [512], P(('group', 'member')), may hold values from 0 to 255, as said below
- prolong_one: float32 [128, 128], replicated, may hold values from -0.5 to 0.5
- slot_two: int32 [256, 5], P(('group', 'member')), may hold values from 0 to 4
- pair_two: int32 [256], P(('group', 'member')), may hold values from 0 to 127, as said below
- prolong_two: float32 [128, 128], replicated, may hold values from -0.5 to 0.5
- diag_inverse: float32 [512, 128, 128], P(('group', 'member')), may hold values from -0.01953125 to 0.01953125
- right_side: float32 [512, 128], P(('group', 'member')), may hold values from -96 to 96
- initial_guess: float32 [512, 128], P(('group', 'member')), may hold values from -6 to 6
Outputs:
- coarse_one: float32 [256, 5, 128, 128], P(('group', 'member'))
- coarse_two: float32 [128, 5, 128, 128], P(('group', 'member'))
- smoothed: float32 [512, 128], P(('group', 'member'))
Inputs may be any that keep to these rules, and one draw needn't show every extreme that they name: Entry 0 of a row is the row's own element; the other four are its neighbours on a periodic grid and lie in the rows of the same device or of the devices just before and just after it in group-major order, cyclically. `pair_one`: every first-level coarse row is named by exactly two fine elements. A fine element names a coarse row held by a device of its own group; the rows of one device name at most 4 rows held by any one device, and some device names exactly 4 rows of some device. `pair_two`: every second-level coarse row is named by exactly two first-level rows. A first-level row names a row held by a device with the same member index; the rows of one device name at most 4 rows held by any one device, and some device names exactly 4 rows of some device.
All inputs are finite; a program needn't handle non-finite values.
Results may differ from a plain program's by a relative error of at most 0.0001.
Values sent between devices are 32-bit elements; how exact they have to be, the bound alone decides.
No kernel may reach another device: no remote copies, remote signals or barrier semaphores. Data moves between devices by JAX's collectives and lax.ppermute only.
A program may use at most 128 MiB of HBM per device.

v0:
```python
import functools

import jax
import jax.numpy as jnp
from jax import lax
from jax.experimental import pallas as pl
from jax.experimental.pallas import tpu as pltpu
from jax.sharding import PartitionSpec as P

damping = 0.7
rows_a_step = 4
prepare_limit = 20 * 1024 * 1024
vmem_limit = 20 * 1024 * 1024
pause = 3
beside = 6


def grid_of(member_count):
    x_count = max(d for d in range(1, member_count + 1) if member_count % d == 0 and d * d <= member_count)
    return member_count // x_count, x_count


def chunk_steps(part):
    tiles = part // 8
    step = max(tiles // 4, 1)
    ends = [max(step // 2, 1)] * min(2, tiles)
    inner = tiles - sum(ends)
    steps = ends[:1] + [step] * (inner // step) + [inner % step] * (inner % step > 0) + ends[1:]
    return [8 * step for step in steps]


def split(values):
    high = values.astype(jnp.bfloat16)
    low = (values - high.astype(jnp.float32)).astype(jnp.bfloat16)
    return high, low


def load_weights(prolong_ref, left_ref, right_ref):
    prolong = prolong_ref[...]
    size = prolong.shape[0]
    high, low = split(prolong)
    high_t, low_t = split(prolong.T)
    for half in range(2):
        at = pl.ds(half * size, size)
        left_ref[0:size, at] = high_t
        left_ref[size : 2 * size, at] = low_t
        right_ref[at, 0:size] = high
        right_ref[at, size : 2 * size] = low


def triple(blocks, left_ref, right_ref):
    size = blocks[0].shape[0]
    count = len(blocks)
    high, low = split(jnp.concatenate(blocks, axis=1))
    both = jnp.dot(
        left_ref[...], jnp.concatenate([high, low], axis=0), preferred_element_type=jnp.float32
    )
    left = both[:size] + both[size:]
    rows = jnp.concatenate([left[:, s * size : (s + 1) * size] for s in range(count)], axis=0)
    high, low = split(rows)
    both = jnp.dot(
        jnp.concatenate([high, low], axis=1), right_ref[...], preferred_element_type=jnp.float32
    )
    return (both[:, :size] + both[:, size:]).reshape(count, size, size)


def prepare_kernel(x_count, slot_ref, place_ref, prolong_ref, fine_ref, *rest):
    outs, (left_ref, right_ref, sums_ref, done_ref) = rest[:-4], rest[-4:]
    held, links, size, _ = fine_ref.shape
    chunks = len(outs) // x_count
    part = size // x_count

    @pl.when(pl.program_id(0) == 0)
    def _():
        load_weights(prolong_ref, left_ref, right_ref)

    sums_ref[...] = jnp.zeros_like(sums_ref)
    for row in range(held):
        for link in range(links):
            slot = slot_ref[pl.program_id(0) * held + row, link]
            sums_ref[row, slot] += fine_ref[row, link]
    sums = [sums_ref[row, slot] for row in range(held) for slot in range(links)]
    done_ref[...] = triple(sums, left_ref, right_ref).reshape(done_ref.shape)
    for offset in range(x_count):
        start = lax.rem(place_ref[0] + offset, x_count) * part
        for out in outs[offset * chunks : (offset + 1) * chunks]:
            step = out.shape[2]
            out[...] = done_ref[:, :, pl.ds(pl.multiple_of(start, 8), step), :]
            start = start + step


def prepare(fine_blocks, slot_one, prolong_one, place, x_count, steps):
    rows, links, size, _ = fine_blocks.shape
    chunks = len(steps)
    held = max(h for h in range(1, rows_a_step + 1) if rows % h == 0)
    outs = pl.pallas_call(
        functools.partial(prepare_kernel, x_count),
        out_shape=[jax.ShapeDtypeStruct((rows, links, step, size), jnp.float32) for step in steps]
        * x_count,
        grid_spec=pltpu.PrefetchScalarGridSpec(
            num_scalar_prefetch=2,
            grid=(rows // held,),
            in_specs=[
                pl.BlockSpec((size, size), lambda e, *_: (0, 0)),
                pl.BlockSpec((held, links, size, size), lambda e, *_: (e, 0, 0, 0)),
            ],
            out_specs=[
                pl.BlockSpec((held, links, step, size), lambda e, *_: (e, 0, 0, 0)) for step in steps
            ]
            * x_count,
            scratch_shapes=[
                pltpu.VMEM((2 * size, 2 * size), jnp.bfloat16),
                pltpu.VMEM((2 * size, 2 * size), jnp.bfloat16),
                pltpu.VMEM((held, links, size, size), jnp.float32),
                pltpu.VMEM((held, links, size, size), jnp.float32),
            ],
        ),
        compiler_params=pltpu.CompilerParams(vmem_limit_bytes=prepare_limit),
        cost_estimate=pl.CostEstimate(
            flops=16 * rows * links * size**3,
            bytes_accessed=8 * rows * links * size**2,
            transcendentals=0,
        ),
        name="prepare",
    )(slot_one, place, prolong_one, fine_blocks)
    return [list(outs[offset * chunks : (offset + 1) * chunks]) for offset in range(x_count)]


def whole(kernel, scalars, arrays, out_shapes, name, work=0, scratch=()):
    return pl.pallas_call(
        kernel,
        out_shape=out_shapes,
        in_specs=[pl.BlockSpec(memory_space=pltpu.SMEM)] * len(scalars)
        + [pl.BlockSpec(memory_space=pltpu.VMEM)] * len(arrays),
        out_specs=[pl.BlockSpec(memory_space=pltpu.VMEM)] * len(out_shapes),
        scratch_shapes=scratch,
        compiler_params=pltpu.CompilerParams(vmem_limit_bytes=vmem_limit),
        cost_estimate=pl.CostEstimate(flops=work * 10**9, bytes_accessed=0, transcendentals=0),
        name=name,
    )(*scalars, *arrays)


def combine_kernel(sources, target_ref, *refs):
    arrays, (far_ref, sums_ref) = refs[:sources], refs[sources:]
    rows = arrays[0].shape[0]
    sums_ref[...] = jnp.zeros_like(sums_ref)
    for source in range(sources):

        def one(row, carry, source=source):
            sums_ref[target_ref[source, row]] += arrays[source][row]
            return carry

        lax.fori_loop(0, rows, one, 0, unroll=True)
    far_ref[...] = sums_ref[0 : far_ref.shape[0]]


def finish_kernel(middle_ref, sums_ref, got_ref, *outs):
    half, rows = got_ref.shape[0], outs[-1].shape[0]
    own = len([out for out in outs if out.shape[0] == rows])
    far, near = outs[:-own], outs[-own:]
    width = own * rows
    for d, out in enumerate(far):
        at = (d + 1) * width
        out[...] = sums_ref[half + at : half + at + width] + got_ref[at : at + width]
    for offset, out in enumerate(near):
        at = offset * rows
        total = sums_ref[half + at : half + at + rows] + got_ref[at : at + rows]
        out[...] = jnp.where(middle_ref[0] > 0, total, 0.0)


def settle_kernel(count, *refs):
    near, far, outs = refs[:count], refs[count:-count], refs[-count:]
    rows = outs[0].shape[0]
    for offset, out in enumerate(outs):
        total = near[offset][...]
        for piece in far:
            total = total + piece[offset * rows : (offset + 1) * rows]
        out[...] = total


def second_kernel(x_count, slot_ref, target_ref, *refs):
    parts, outs, sums_ref = refs[:x_count], refs[x_count:-1], refs[-1]
    rows, links, step, _ = parts[0].shape
    share = outs[0].shape[0]
    sums_ref[...] = jnp.zeros_like(sums_ref)

    def one(row, carry):
        target = target_ref[row]
        for link in range(links):
            slot = slot_ref[row, link]
            for offset, part in enumerate(parts):
                sums_ref[target, slot, offset * step : (offset + 1) * step, :] += part[row, link]
        return carry

    lax.fori_loop(0, rows, one, 0, unroll=True)
    for way, out in enumerate(outs):
        out[...] = sums_ref[way * share : (way + 1) * share]


def place_kernel(x_count, place_ref, *refs):
    pieces, out = refs[:-1], refs[-1]
    part = out.shape[2] // x_count
    chunks = len(pieces) // x_count
    for offset in range(x_count):
        start = lax.rem(place_ref[0] + x_count - offset, x_count) * part
        for piece in pieces[offset * chunks : (offset + 1) * chunks]:
            step = piece.shape[2]
            out[:, :, pl.ds(pl.multiple_of(start, 8), step), :] = piece[...]
            start = start + step


def place_one(pieces, place, x_count):
    rows, links, _, size = pieces[0].shape
    return pl.pallas_call(
        functools.partial(place_kernel, x_count),
        out_shape=jax.ShapeDtypeStruct((rows, links, size, size), jnp.float32),
        grid_spec=pltpu.PrefetchScalarGridSpec(
            num_scalar_prefetch=1,
            grid=(rows,),
            in_specs=[
                pl.BlockSpec((1, links, piece.shape[2], size), lambda e, *_: (e, 0, 0, 0))
                for piece in pieces
            ],
            out_specs=pl.BlockSpec((1, links, size, size), lambda e, *_: (e, 0, 0, 0)),
        ),
        compiler_params=pltpu.CompilerParams(vmem_limit_bytes=vmem_limit),
        cost_estimate=pl.CostEstimate(
            flops=0, bytes_accessed=8 * rows * links * size**2, transcendentals=0
        ),
        name="place_one",
    )(place, *pieces)


def last_kernel(x_count, peers, place_ref, prolong_ref, *refs):
    pieces, (out, left_ref, right_ref, sums_ref) = refs[:-4], refs[-4:]
    links, size = out.shape[1], out.shape[2]
    part = size // x_count

    @pl.when(pl.program_id(0) == 0)
    def _():
        load_weights(prolong_ref, left_ref, right_ref)

    done = 0
    for first in range(0, len(pieces), peers):
        total = pieces[first][...]
        for piece in pieces[first + 1 : first + peers]:
            total = total + piece[...]
        step = total.shape[2] // x_count
        for offset in range(x_count):
            start = lax.rem(place_ref[0] + x_count - offset, x_count) * part
            at = pl.multiple_of(start + done, 8)
            sums_ref[:, :, pl.ds(at, step), :] = total[:, :, offset * step : (offset + 1) * step, :]
        done += step
    sums = [sums_ref[row, slot] for row in range(out.shape[0]) for slot in range(links)]
    out[...] = triple(sums, left_ref, right_ref).reshape(out.shape)


def last(pieces, prolong_two, place, x_count, peers):
    rows, links, _, size = pieces[0].shape
    held = max(h for h in range(1, rows_a_step // 2 + 1) if rows % h == 0)
    return pl.pallas_call(
        functools.partial(last_kernel, x_count, peers),
        out_shape=jax.ShapeDtypeStruct((rows, links, size, size), jnp.float32),
        grid_spec=pltpu.PrefetchScalarGridSpec(
            num_scalar_prefetch=1,
            grid=(rows // held,),
            in_specs=[pl.BlockSpec((size, size), lambda e, *_: (0, 0))]
            + [
                pl.BlockSpec((held, links, piece.shape[2], size), lambda e, *_: (e, 0, 0, 0))
                for piece in pieces
            ],
            out_specs=pl.BlockSpec((held, links, size, size), lambda e, *_: (e, 0, 0, 0)),
            scratch_shapes=[
                pltpu.VMEM((2 * size, 2 * size), jnp.bfloat16),
                pltpu.VMEM((2 * size, 2 * size), jnp.bfloat16),
                pltpu.VMEM((held, links, size, size), jnp.float32),
            ],
        ),
        compiler_params=pltpu.CompilerParams(vmem_limit_bytes=vmem_limit),
        cost_estimate=pl.CostEstimate(
            flops=16 * rows * links * size**3,
            bytes_accessed=4 * rows * links * size**2 * (peers + 1),
            transcendentals=0,
        ),
        name="last",
    )(place, prolong_two, *pieces)


def sweep(fine_blocks, neighbours, diag_inverse, right_side, initial_guess):
    rows = fine_blocks.shape[0]
    axes = ("group", "member")
    devices = lax.axis_size(axes)
    device = lax.axis_index(axes)
    before = lax.ppermute(initial_guess, axes, [(i, (i + 1) % devices) for i in range(devices)])
    after = lax.ppermute(initial_guess, axes, [(i, (i - 1) % devices) for i in range(devices)])
    window = jnp.concatenate([before, initial_guess, after], axis=0)
    position = (neighbours - device * rows + rows) % (rows * devices)
    nearby = window[position]
    product = jnp.sum(fine_blocks * nearby[:, :, None, :], axis=(1, 3))
    defect = right_side - product
    return initial_guess + damping * jnp.sum(diag_inverse * defect[:, None, :], axis=2)


def local(
    fine_blocks,
    neighbours,
    slot_one,
    pair_one,
    prolong_one,
    slot_two,
    pair_two,
    prolong_two,
    diag_inverse,
    right_side,
    initial_guess,
):
    rows, links, size, _ = fine_blocks.shape
    rows_one, rows_two = rows // 2, rows // 4
    members, groups = lax.axis_size("member"), lax.axis_size("group")
    z_count, x_count = grid_of(members)
    half = z_count // 2
    part = size // x_count
    steps = chunk_steps(part)

    member = lax.axis_index("member")
    z, x = member // x_count, member % x_count
    upper = (z >= half).astype(jnp.int32)
    place = jnp.stack([x]).astype(jnp.int32)

    def at(side, d, x_at):
        return (half + d if side else half - 1 - d) * x_count + x_at % x_count

    def hop(array, d_from, d_to, offset):
        pairs = [
            (at(side, d_from, x_at), at(side, d_to, x_at + offset))
            for side in range(2)
            for x_at in range(x_count)
        ]
        return lax.ppermute(array, "member", pairs)

    def hop_x(array, offset):
        pairs = [
            (z_at * x_count + x_at, z_at * x_count + (x_at + offset) % x_count)
            for z_at in range(z_count)
            for x_at in range(x_count)
        ]
        return lax.ppermute(array, "member", pairs)

    routes = [(d, o) for d in range(half) for o in range(x_count)]

    def along(arrays):
        return [array if o == 0 else hop_x(array, o) for o, array in enumerate(arrays)]

    def inward(arrays):
        return arrays + [hop(array, d, 0, 0) for d in range(1, half) for array in arrays]

    tags = jnp.stack(along([pair_one] * x_count))
    slot_one, tags = lax.optimization_barrier((slot_one, tags))
    owner_rows = jnp.concatenate([tags] + [hop(tags, d, 0, 0) for d in range(1, half)])
    owner = owner_rows // rows_one % members
    owner_z, owner_x = owner // x_count, owner % x_count
    owner_upper = (owner_z >= half).astype(jnp.int32)
    owner_d = jnp.where(owner_upper > 0, owner_z - half, half - 1 - owner_z)
    near = (owner_upper == upper).astype(jnp.int32)
    target_one = ((near * half + owner_d) * x_count + (owner_x - x + x_count) % x_count) * rows_one
    target_one = (target_one + owner_rows % rows_one).astype(jnp.int32)
    middle = jnp.stack([(z == half - 1) | (z == half)]).astype(jnp.int32)

    way = (pair_two // rows_two // members - lax.axis_index("group") + groups) % groups
    target_two = (way * rows_two + pair_two % rows_two).astype(jnp.int32)

    outgoing = prepare(fine_blocks, slot_one, prolong_one, place, x_count, steps)
    across = [(at(0, 0, x_at), at(1, 0, x_at)) for x_at in range(x_count)]
    across = across + [(b, a) for a, b in across]
    before = [target_one]

    def in_turn(kernel, scalars, arrays, out_shapes, name, **more):
        arrays, before[0] = lax.optimization_barrier((list(arrays), before[0]))
        outs = whole(kernel, scalars, arrays, out_shapes, name, **more)
        before[0] = outs[0]
        return outs

    def rows_of(count, height):
        return jax.ShapeDtypeStruct((count, links, height, size), jnp.float32)

    coming, targets = [], [target_one]
    for chunk in range(len(steps)):
        own = outgoing[0][chunk]
        if chunk > 0:
            ahead = coming[-1]
            tied = (own, ahead[x_count], targets[0]) if chunk == 1 else (own, ahead[x_count])
            own, ahead[x_count], *seen = lax.optimization_barrier(tied)
            targets += seen
        coming.append(inward(along([own] + [ways[chunk] for ways in outgoing[1:]])))
    received = []

    smoothed = []

    def combine(chunk):
        held = coming[chunk]
        if chunk == min(1, len(steps) - 1):
            later, before[0] = lax.optimization_barrier((neighbours, before[0]))
            swept = sweep(fine_blocks, later, diag_inverse, right_side, initial_guess)
            held, swept = lax.optimization_barrier((held, swept))
            smoothed.append(swept)
        total = half * x_count * rows_one
        far, kept = in_turn(
            functools.partial(combine_kernel, len(held)),
            [targets[min(chunk, 1)]],
            held,
            [rows_of(total, steps[chunk]), rows_of(2 * total, steps[chunk])],
            "combine",
            work=beside,
        )
        return kept, lax.ppermute(far, "member", across)

    def finish(chunk, sums):
        finished = in_turn(
            finish_kernel,
            [middle],
            sums,
            [rows_of(x_count * rows_one, steps[chunk])] * (half - 1)
            + [rows_of(rows_one, steps[chunk])] * x_count,
            "finish",
        )
        return list(finished[half - 1 :]) + [hop(finished[d - 1], 0, d, 0) for d in range(1, half)]

    def settle(chunk, finished):
        return along(
            in_turn(
                functools.partial(settle_kernel, x_count),
                [],
                finished,
                [rows_of(rows_one, steps[chunk])] * x_count,
                "settle",
            )
        )

    def second(chunk, ours):
        received[-groups:], ours = lax.optimization_barrier((received[-groups:], ours))
        height = x_count * steps[chunk]
        shares = in_turn(
            functools.partial(second_kernel, x_count),
            [slot_two, target_two],
            ours,
            [rows_of(rows_two, height)] * groups,
            "second",
            scratch=[pltpu.VMEM((groups * rows_two, links, height, size), jnp.float32)],
        )
        for way, share in enumerate(shares):
            around = [(g, (g + way) % groups) for g in range(groups)]
            received.append(lax.ppermute(share, "group", around) if way > 0 else share)
        return ours

    stages, shares = (combine, finish, settle, second), (1.0, 0.5, 0.25)
    turns, rows_in, swapped = [], 0.0, 0.0
    for chunk, step in enumerate(steps):
        rows_in += step
        time = swapped = max(rows_in, swapped) + step + pause
        turns += [(rows_in, 0, chunk), (time, 1, chunk)]
        for stage, share in enumerate(shares[1:], 2):
            time += share * step + pause
            turns.append((time, stage, chunk))
    held = [[None] * len(steps) for _ in range(len(stages) + 1)]
    for _, stage, chunk in sorted(turns):
        given = [held[stage][chunk]] if stage > 0 else []
        held[stage + 1][chunk] = stages[stage](chunk, *given)
    parts = held[4]

    coarse_one = place_one(
        [parts[chunk][o] for o in range(x_count) for chunk in range(len(steps))], place, x_count
    )
    coarse_two = last(received, prolong_two, place, x_count, groups)
    return (coarse_one, coarse_two, smoothed[0])


def solution(mesh):
    rows = P(("group", "member"))
    return jax.shard_map(
        local,
        mesh=mesh,
        in_specs=(rows, rows, rows, rows, P(), rows, rows, P(), rows, rows, rows),
        out_specs=(rows, rows, rows),
        check_vma=False,
    )
```

profile of v0, /device:TPU:0, one launch (start us, length us, event | category | flops | bytes accessed | tf_op | source)
XLA Modules:
  0.0 233.6 jit_solution(14506886746527906266)
XLA Ops:
  0.6 3.0 %collective-permute-start = (s32[16]{0:T(128)}, s32[16]{0:T(128)S(1)}, u32[]{:S(2)}, u32[]{:S(2)}) collective-permute-start(s32[16]{0:T(128)} %param.14), channel_id=1, source_target_pairs={{0,1},{1,0},{2,3},{3,2},{4,5},{5,4},{6,7},{7,6},{8,9},{9,8},{10,11... | collective-permute-start | bytes 200 | tf_op jit(solution)/shard_map/ppermute | solution.py:347
  3.6 1.7 collective-permute-done
  6.7 2.5 %copy-done = f32[16,5,128,128]{3,2,1,0:T(8,128)S(1)} copy-done((f32[16,5,128,128]{3,2,1,0:T(8,128)S(1)}, f32[16,5,128,128]{3,2,1,0:T(8,128)}, u32[]{:S(2)}) %copy-start) | copy-done | bytes 5242904
  10.0 6.8 %prepare.1 = (f32[16,5,8,128]{3,2,1,0:T(8,128)S(1)}, f32[16,5,16,128]{3,2,1,0:T(8,128)S(1)}, f32[16,5,16,128]{3,2,1,0:T(8,128)S(1)}, f32[16,5,16,128]{3,2,1,0:T(...) custom-call(s32[16,5]{1,0:T(8,128)S(1)} %copy.16.slot_ref, ...), custom_call_target="tpu_custom_call" | custom-call | flops 2684354560 | bytes 10485760 | tf_op jit(solution)/shard_map/prepare/pallas_call | solution.py:96
  20.0 2.0 collective-permute-start.2
  22.0 3.5 %collective-permute-start.3 = (f32[16,5,8,128]{3,2,1,0:T(8,128)S(1)}, f32[16,5,8,128]{3,2,1,0:T(8,128)S(1)}, u32[]{:S(2)}, u32[]{:S(2)}) collective-permute-start(f32[16,5,8,128]{3,2,1,0:T(8,128)S(1)} %get-tuple-element.172.refs_0_), channel_id=1, source_target_pairs={{0,2},{1,3},{6,4},{7,5},{8,10},{9,11},{14,12},{15,13},{16,18},{17,... | collective-permute-start | bytes 983048 | tf_op jit(solution)/shard_map/ppermute | solution.py:339
  25.5 3.1 %collective-permute-done.2.refs_1_ = f32[16,5,8,128]{3,2,1,0:T(8,128)S(1)} collective-permute-done((f32[16,5,8,128]{3,2,1,0:T(8,128)S(1)}, f32[16,5,8,128]{3,2,1,0:T(8,128)S(1)}, u32[]{:S(2)}, u32[]{:S(2)}) %collective-permute-start.2) | collective-permute-done | bytes 327712 | tf_op jit(solution)/shard_map/ppermute | solution.py:347
  28.6 3.7 %collective-permute-start.4 = (f32[16,5,8,128]{3,2,1,0:T(8,128)S(1)}, f32[16,5,8,128]{3,2,1,0:T(8,128)S(1)}, u32[]{:S(2)}, u32[]{:S(2)}) collective-permute-start(f32[16,5,8,128]{3,2,1,0:T(8,128)S(1)} %collective-permute-done.2.refs_1_), channel_id=1, source_target_pairs={{0,2},{1,3},{6,4},{7,5},{8,10},{9,11},{14,12},{15,13},{16,18},{17,... | collective-permute-start | bytes 983048 | tf_op jit(solution)/shard_map/ppermute | solution.py:339
  33.6 1.6 collective-permute-start.7
  35.2 2.9 %collective-permute-done.1 = s32[2,16]{1,0:T(2,128)S(1)} collective-permute-done((s32[2,16]{1,0:T(2,128)S(1)}, s32[2,16]{1,0:T(2,128)S(1)}, u32[]{:S(2)}, u32[]{:S(2)}) %collective-permute-start.1) | collective-permute-done | bytes 160 | tf_op jit(solution)/shard_map/ppermute | solution.py:339
  38.8 5.2 %collective-permute-start.8 = (f32[16,5,16,128]{3,2,1,0:T(8,128)S(1)}, f32[16,5,16,128]{3,2,1,0:T(8,128)}, u32[]{:S(2)}, u32[]{:S(2)}) collective-permute-start(f32[16,5,16,128]{3,2,1,0:T(8,128)S(1)} %get-tuple-element.193.refs_0_), channel_id=1, source_target_pairs={{0,2},{1,3},{6,4},{7,5},{8,10},{9,11},{14,12},{15,13},{16,18},{17,... | collective-permute-start | bytes 1966088 | tf_op jit(solution)/shard_map/ppermute | solution.py:339
  46.8 1.9 combine.5
  49.6 2.0 collective-permute-start.10
  51.6 3.7 %collective-permute-done.11 = f32[16,128]{1,0:T(8,128)S(1)} collective-permute-done((f32[16,128]{1,0:T(8,128)S(1)}, f32[16,128]{1,0:T(8,128)S(1)}, u32[]{:S(2)}, u32[]{:S(2)}) %collective-permute-start.11) | collective-permute-done | bytes 8224 | tf_op jit(solution)/shard_map/ppermute | solution.py:295
  56.5 11.9 %collective-permute-start.9 = (f32[16,5,16,128]{3,2,1,0:T(8,128)}, f32[16,5,16,128]{3,2,1,0:T(8,128)}, u32[]{:S(2)}, u32[]{:S(2)}) collective-permute-start(f32[16,5,16,128]{3,2,1,0:T(8,128)} %collective-permute-done.7.refs_1_), channel_id=1, source_target_pairs={{0,2},{1,3},{6,4},{7,5},{8,10},{9,11},{14,12},{15,13},{16,18},{17,... | collective-permute-start | bytes 1966088 | tf_op jit(solution)/shard_map/ppermute | solution.py:339
  69.3 3.1 %multiply_reduce_fusion = f32[16,128]{1,0:T(8,128)S(1)} fusion(f32[16,5,128,128]{3,2,1,0:T(8,128)} %fine_ref.1, f32[16,5,128]{2,1,0:T(8,128)S(1)} %reshape.12), kind=kLoop, calls=%fused_computation.1 | loop fusion | flops 2619392 | bytes 5292032 | tf_op jit(solution)/shard_map/reduce_sum | solution.py:299
  73.4 4.7 %collective-permute-done.9.refs_3_ = f32[16,5,16,128]{3,2,1,0:T(8,128)} collective-permute-done((f32[16,5,16,128]{3,2,1,0:T(8,128)}, f32[16,5,16,128]{3,2,1,0:T(8,128)}, u32[]{:S(2)}, u32[]{:S(2)}) %collective-permute-start.9) | collective-permute-done | bytes 655392 | tf_op jit(solution)/shard_map/ppermute | solution.py:339
  78.1 2.2 combine.6
  81.1 5.5 %collective-permute-start.18 = (f32[16,5,16,128]{3,2,1,0:T(8,128)S(1)}, f32[16,5,16,128]{3,2,1,0:T(8,128)S(1)}, u32[]{:S(2)}, u32[]{:S(2)}) collective-permute-start(f32[16,5,16,128]{3,2,1,0:T(8,128)S(1)} %copy-done.6), channel_id=1, source_target_pairs={{0,2},{1,3},{6,4},{7,5},{8,10},{9,11},{14,12},{15,13},{16,18},{17,... | collective-permute-start | bytes 1966088 | tf_op jit(solution)/shard_map/ppermute | solution.py:339
  89.7 7.2 %collective-permute-done.6.refs_2_ = f32[16,5,8,128]{3,2,1,0:T(8,128)S(1)} collective-permute-done((f32[16,5,8,128]{3,2,1,0:T(8,128)S(1)}, f32[16,5,8,128]{3,2,1,0:T(8,128)S(1)}, u32[]{:S(2)}, u32[]{:S(2)}) %collective-permute-start.6) | collective-permute-done | bytes 327712 | tf_op jit(solution)/shard_map/ppermute | solution.py:339
  97.4 4.3 %collective-permute-done.18.refs_2_ = f32[16,5,16,128]{3,2,1,0:T(8,128)S(1)} collective-permute-done((f32[16,5,16,128]{3,2,1,0:T(8,128)S(1)}, f32[16,5,16,128]{3,2,1,0:T(8,128)S(1)}, u32[]{:S(2)}, u32[]{:S(2)}) %collective-permute-start.18) | collective-permute-done | bytes 655392 | tf_op jit(solution)/shard_map/ppermute | solution.py:339
  101.7 4.4 %collective-permute-start.23 = (f32[16,5,16,128]{3,2,1,0:T(8,128)S(1)}, f32[16,5,16,128]{3,2,1,0:T(8,128)S(1)}, u32[]{:S(2)}, u32[]{:S(2)}) collective-permute-start(f32[16,5,16,128]{3,2,1,0:T(8,128)S(1)} %get-tuple-element.237.refs_0_), channel_id=1, source_target_pairs={{0,2},{1,3},{6,4},{7,5},{8,10},{9,11},{14,12},{15,13},{16,18},{17,... | collective-permute-start | bytes 1966088 | tf_op jit(solution)/shard_map/ppermute | solution.py:339
  107.0 8.9 %collective-permute-done.19.refs_3_ = f32[16,5,16,128]{3,2,1,0:T(8,128)S(1)} collective-permute-done((f32[16,5,16,128]{3,2,1,0:T(8,128)}, f32[16,5,16,128]{3,2,1,0:T(8,128)S(1)}, u32[]{:S(2)}, u32[]{:S(2)}) %collective-permute-start.19) | collective-permute-done | bytes 655392 | tf_op jit(solution)/shard_map/ppermute | solution.py:339
  115.8 1.8 combine.7
  119.1 4.6 %collective-permute-start.24 = (f32[16,5,16,128]{3,2,1,0:T(8,128)S(1)}, f32[16,5,16,128]{3,2,1,0:T(8,128)S(1)}, u32[]{:S(2)}, u32[]{:S(2)}) collective-permute-start(f32[16,5,16,128]{3,2,1,0:T(8,128)S(1)} %collective-permute-done.22.refs_1_), channel_id=1, source_target_pairs={{0,2},{1,3},{6,4},{7,5},{8,10},{9,11},{14,12},{15,13},{16,18},{17,... | collective-permute-start | bytes 1966088 | tf_op jit(solution)/shard_map/ppermute | solution.py:339
  125.0 4.8 %collective-permute-done.23.refs_2_ = f32[16,5,16,128]{3,2,1,0:T(8,128)S(1)} collective-permute-done((f32[16,5,16,128]{3,2,1,0:T(8,128)S(1)}, f32[16,5,16,128]{3,2,1,0:T(8,128)S(1)}, u32[]{:S(2)}, u32[]{:S(2)}) %collective-permute-start.23) | collective-permute-done | bytes 655392 | tf_op jit(solution)/shard_map/ppermute | solution.py:339
  130.3 1.5 collective-permute-start.14
  131.9 6.2 %collective-permute-done.24.refs_3_ = f32[16,5,16,128]{3,2,1,0:T(8,128)S(1)} collective-permute-done((f32[16,5,16,128]{3,2,1,0:T(8,128)S(1)}, f32[16,5,16,128]{3,2,1,0:T(8,128)S(1)}, u32[]{:S(2)}, u32[]{:S(2)}) %collective-permute-start.24) | collective-permute-done | bytes 655392 | tf_op jit(solution)/shard_map/ppermute | solution.py:339
  140.7 7.2 %collective-permute-start.32 = (f32[16,5,8,128]{3,2,1,0:T(8,128)S(1)}, f32[16,5,8,128]{3,2,1,0:T(8,128)S(1)}, u32[]{:S(2)}, u32[]{:S(2)}) collective-permute-start(f32[16,5,8,128]{3,2,1,0:T(8,128)S(1)} %collective-permute-done.30.refs_1_), channel_id=1, source_target_pairs={{0,2},{1,3},{6,4},{7,5},{8,10},{9,11},{14,12},{15,13},{16,18},{17,... | collective-permute-start | bytes 983048 | tf_op jit(solution)/shard_map/ppermute | solution.py:339
  151.8 4.3 %collective-permute-done.32.refs_3_ = f32[16,5,8,128]{3,2,1,0:T(8,128)S(1)} collective-permute-done((f32[16,5,8,128]{3,2,1,0:T(8,128)S(1)}, f32[16,5,8,128]{3,2,1,0:T(8,128)S(1)}, u32[]{:S(2)}, u32[]{:S(2)}) %collective-permute-start.32) | collective-permute-done | bytes 327712 | tf_op jit(solution)/shard_map/ppermute | solution.py:339
  156.0 1.5 collective-permute-start.26
  157.5 4.4 %collective-permute-done.31.refs_2_ = f32[16,5,8,128]{3,2,1,0:T(8,128)S(1)} collective-permute-done((f32[16,5,8,128]{3,2,1,0:T(8,128)S(1)}, f32[16,5,8,128]{3,2,1,0:T(8,128)S(1)}, u32[]{:S(2)}, u32[]{:S(2)}) %collective-permute-start.31) | collective-permute-done | bytes 327712 | tf_op jit(solution)/shard_map/ppermute | solution.py:339
  163.1 5.4 %collective-permute-done.29.refs_2_ = f32[16,5,16,128]{3,2,1,0:T(8,128)S(1)} collective-permute-done((f32[16,5,16,128]{3,2,1,0:T(8,128)S(1)}, f32[16,5,16,128]{3,2,1,0:T(8,128)S(1)}, u32[]{:S(2)}, u32[]{:S(2)}) %collective-permute-start.29) | collective-permute-done | bytes 655392 | tf_op jit(solution)/shard_map/ppermute | solution.py:339
  168.6 1.5 collective-permute-start.33
  170.9 6.1 %collective-permute-done.33.refs_1_.refs_7_ = f32[8,5,16,128]{3,2,1,0:T(8,128)S(1)} collective-permute-done((f32[8,5,16,128]{3,2,1,0:T(8,128)S(1)}, f32[8,5,16,128]{3,2,1,0:T(8,128)S(1)}, u32[]{:S(2)}, u32[]{:S(2)}) %collective-permute-start.33) | collective-permute-done | bytes 327712 | tf_op jit(solution)/shard_map/ppermute | solution.py:347
  179.5 1.6 collective-permute-start.35
  183.8 13.8 %collective-permute-done.38.refs_2_ = f32[16,5,16,128]{3,2,1,0:T(8,128)S(1)} collective-permute-done((f32[16,5,16,128]{3,2,1,0:T(8,128)S(1)}, f32[16,5,16,128]{3,2,1,0:T(8,128)S(1)}, u32[]{:S(2)}, u32[]{:S(2)}) %collective-permute-start.38) | collective-permute-done | bytes 655392 | tf_op jit(solution)/shard_map/ppermute | solution.py:339
  197.7 1.5 collective-permute-start.40
  199.3 2.2 collective-permute-done.41.refs_2_
  201.5 3.4 %collective-permute-done.40.refs_1_.refs_8_ = f32[8,5,16,128]{3,2,1,0:T(8,128)S(1)} collective-permute-done((f32[8,5,16,128]{3,2,1,0:T(8,128)S(1)}, f32[8,5,16,128]{3,2,1,0:T(8,128)S(1)}, u32[]{:S(2)}, u32[]{:S(2)}) %collective-permute-start.40) | collective-permute-done | bytes 327712 | tf_op jit(solution)/shard_map/ppermute | solution.py:347
  205.9 1.6 collective-permute-start.43
  208.8 1.5 collective-permute-start.45
  210.3 3.8 %collective-permute-done.45.refs_9_.refs_1_ = f32[8,5,8,128]{3,2,1,0:T(8,128)S(1)} collective-permute-done((f32[8,5,8,128]{3,2,1,0:T(8,128)S(1)}, f32[8,5,8,128]{3,2,1,0:T(8,128)S(1)}, u32[]{:S(2)}, u32[]{:S(2)}) %collective-permute-start.45) | collective-permute-done | bytes 163872 | tf_op jit(solution)/shard_map/ppermute | solution.py:347
  216.5 5.4 %collective-permute-done.44.refs_15_ = f32[4,5,32,128]{3,2,1,0:T(8,128)S(1)} collective-permute-done((f32[4,5,32,128]{3,2,1,0:T(8,128)S(1)}, f32[4,5,32,128]{3,2,1,0:T(8,128)S(1)}, u32[]{:S(2)}, u32[]{:S(2)}) %collective-permute-start.44) | collective-permute-done | bytes 327712 | tf_op jit(solution)/shard_map/ppermute | solution.py:452
  223.6 1.5 collective-permute-start.47
  225.1 3.1 %place_one.1 = f32[8,5,128,128]{3,2,1,0:T(8,128)} custom-call(s32[1]{0:T(128)} %bitcast.place_ref, f32[8,5,8,128]{3,2,1,0:T(8,128)S(1)} %get-tuple-element.205.refs_0_, f32[8,5,16,128]{3,2,1,0:T(8,128)S(1)} %get-tuple-element.242.refs_0_.refs_1_, f32[8,5,16,128]{3,2,1,0:T(8,128)S(1)} %get-tuple-element.268.refs_0_.refs_2_, ...), custom_call_target="tpu_custom_call" | custom-call | bytes 5242880 | tf_op jit(solution)/shard_map/place_one/pallas_call | solution.py:214
  228.3 2.5 %collective-permute-done.47.refs_18_ = f32[4,5,16,128]{3,2,1,0:T(8,128)S(1)} collective-permute-done((f32[4,5,16,128]{3,2,1,0:T(8,128)S(1)}, f32[4,5,16,128]{3,2,1,0:T(8,128)S(1)}, u32[]{:S(2)}, u32[]{:S(2)}) %collective-permute-start.47) | collective-permute-done | bytes 163872 | tf_op jit(solution)/shard_map/ppermute | solution.py:452
  231.1 2.6 %last.1 = f32[4,5,128,128]{3,2,1,0:T(8,128)} custom-call(s32[1]{0:T(128)} %bitcast.place_ref, f32[128,128]{1,0:T(8,128)S(1)} %copy-done.2, f32[4,5,16,128]{3,2,1,0:T(8,128)S(1)} %get-tuple-element.306.refs_0_, f32[4,5,16,128]{3,2,1,0:T(8,128)S(1)} %collective-permute-done.13.refs_1_, f32[4,5,16,128]{3,2,1,0:T(8,128)S(1)} %collective-permute-done.14.refs_2_, ...), custom_call_target="tpu_custom_call" | custom-call | flops 671088640 | bytes 6553600 | tf_op jit(solution)/shard_map/last/pallas_call | solution.py:261
  (134 shorter events, 42.9 us)
Async XLA Ops:
  20.0 8.6 %collective-permute-start.2 = (f32[16,5,8,128]{3,2,1,0:T(8,128)S(1)}, f32[16,5,8,128]{3,2,1,0:T(8,128)S(1)}, u32[]{:S(2)}, u32[]{:S(2)}) collective-permute-start(f32[16,5,8,128]{3,2,1,0:T(8,128)S(1)} %get-tuple-element.169), channel_id=1, source_target_pairs={{0,1},{1,0},{2,3},{3,2},{4,5},{5,4},{6,7},{7,6},{8,9},{9,8},{10,11... | collective-permute-start | bytes 983048 | tf_op jit(solution)/shard_map/ppermute | solution.py:347
  22.0 16.1 %collective-permute-start.3 = (f32[16,5,8,128]{3,2,1,0:T(8,128)S(1)}, f32[16,5,8,128]{3,2,1,0:T(8,128)S(1)}, u32[]{:S(2)}, u32[]{:S(2)}) collective-permute-start(f32[16,5,8,128]{3,2,1,0:T(8,128)S(1)} %get-tuple-element.172.refs_0_), channel_id=1, source_target_pairs={{0,2},{1,3},{6,4},{7,5},{8,10},{9,11},{14,12},{15,13},{16,18},{17,... | collective-permute-start | bytes 983048 | tf_op jit(solution)/shard_map/ppermute | solution.py:339
  28.6 15.5 %collective-permute-start.4 = (f32[16,5,8,128]{3,2,1,0:T(8,128)S(1)}, f32[16,5,8,128]{3,2,1,0:T(8,128)S(1)}, u32[]{:S(2)}, u32[]{:S(2)}) collective-permute-start(f32[16,5,8,128]{3,2,1,0:T(8,128)S(1)} %collective-permute-done.2.refs_1_), channel_id=1, source_target_pairs={{0,2},{1,3},{6,4},{7,5},{8,10},{9,11},{14,12},{15,13},{16,18},{17,... | collective-permute-start | bytes 983048 | tf_op jit(solution)/shard_map/ppermute | solution.py:339
  32.3 5.8 %collective-permute-start.1 = (s32[2,16]{1,0:T(2,128)S(1)}, s32[2,16]{1,0:T(2,128)S(1)}, u32[]{:S(2)}, u32[]{:S(2)}) collective-permute-start(s32[2,16]{1,0:T(2,128)S(1)} %pad_add_fusion.1), channel_id=1, source_target_pairs={{0,2},{1,3},{6,4},{7,5},{8,10},{9,11},{14,12},{15,13},{16,18},{17,... | collective-permute-start | bytes 392 | tf_op jit(solution)/shard_map/ppermute | solution.py:339
  33.6 22.9 %collective-permute-start.7 = (f32[16,5,16,128]{3,2,1,0:T(8,128)}, f32[16,5,16,128]{3,2,1,0:T(8,128)}, u32[]{:S(2)}, u32[]{:S(2)}) collective-permute-start(f32[16,5,16,128]{3,2,1,0:T(8,128)} %get-tuple-element.185), channel_id=1, source_target_pairs={{0,1},{1,0},{2,3},{3,2},{4,5},{5,4},{6,7},{7,6},{8,9},{9,8},{10,11... | collective-permute-start | bytes 1966088 | tf_op jit(solution)/shard_map/ppermute | solution.py:347
  38.8 29.5 %collective-permute-start.8 = (f32[16,5,16,128]{3,2,1,0:T(8,128)S(1)}, f32[16,5,16,128]{3,2,1,0:T(8,128)}, u32[]{:S(2)}, u32[]{:S(2)}) collective-permute-start(f32[16,5,16,128]{3,2,1,0:T(8,128)S(1)} %get-tuple-element.193.refs_0_), channel_id=1, source_target_pairs={{0,2},{1,3},{6,4},{7,5},{8,10},{9,11},{14,12},{15,13},{16,18},{17,... | collective-permute-start | bytes 1966088 | tf_op jit(solution)/shard_map/ppermute | solution.py:339
  48.7 19.7 %collective-permute-start.5 = (f32[32,5,8,128]{3,2,1,0:T(8,128)}, f32[32,5,8,128]{3,2,1,0:T(8,128)S(1)}, u32[]{:S(2)}, u32[]{:S(2)}) collective-permute-start(f32[32,5,8,128]{3,2,1,0:T(8,128)} %get-tuple-element.177), channel_id=1, source_target_pairs={{2,4},{3,5},{4,2},{5,3},{10,12},{11,13},{12,10},{13,11},{18,20},{1... | collective-permute-start | bytes 1966088 | tf_op jit(solution)/shard_map/ppermute | solution.py:415
  49.5 5.8 %collective-permute-start.11 = (f32[16,128]{1,0:T(8,128)S(1)}, f32[16,128]{1,0:T(8,128)S(1)}, u32[]{:S(2)}, u32[]{:S(2)}) collective-permute-start(f32[16,128]{1,0:T(8,128)S(1)} %copy-done.19), channel_id=1, source_target_pairs={{0,31},{1,0},{2,1},{3,2},{4,3},{5,4},{6,5},{7,6},{8,7},{9,8},{10,9... | collective-permute-start | bytes 24584 | tf_op jit(solution)/shard_map/ppermute | solution.py:295
  49.6 6.9 %collective-permute-start.10 = (f32[16,128]{1,0:T(8,128)S(1)}, f32[16,128]{1,0:T(8,128)S(1)}, u32[]{:S(2)}, u32[]{:S(2)}) collective-permute-start(f32[16,128]{1,0:T(8,128)S(1)} %copy-done.19), channel_id=1, source_target_pairs={{0,1},{1,2},{2,3},{3,4},{4,5},{5,6},{6,7},{7,8},{8,9},{9,10},{10,1... | collective-permute-start | bytes 24584 | tf_op jit(solution)/shard_map/ppermute | solution.py:294
  55.3 31.2 %collective-permute-start.17 = (f32[16,5,16,128]{3,2,1,0:T(8,128)}, f32[16,5,16,128]{3,2,1,0:T(8,128)}, u32[]{:S(2)}, u32[]{:S(2)}) collective-permute-start(f32[16,5,16,128]{3,2,1,0:T(8,128)} %get-tuple-element.213), channel_id=1, source_target_pairs={{0,1},{1,0},{2,3},{3,2},{4,5},{5,4},{6,7},{7,6},{8,9},{9,8},{10,11... | collective-permute-start | bytes 1966088 | tf_op jit(solution)/shard_map/ppermute | solution.py:347
  56.5 21.6 %collective-permute-start.9 = (f32[16,5,16,128]{3,2,1,0:T(8,128)}, f32[16,5,16,128]{3,2,1,0:T(8,128)}, u32[]{:S(2)}, u32[]{:S(2)}) collective-permute-start(f32[16,5,16,128]{3,2,1,0:T(8,128)} %collective-permute-done.7.refs_1_), channel_id=1, source_target_pairs={{0,2},{1,3},{6,4},{7,5},{8,10},{9,11},{14,12},{15,13},{16,18},{17,... | collective-permute-start | bytes 1966088 | tf_op jit(solution)/shard_map/ppermute | solution.py:339
  80.3 37.3 %collective-permute-start.16 = (f32[32,5,16,128]{3,2,1,0:T(8,128)S(1)}, f32[32,5,16,128]{3,2,1,0:T(8,128)S(1)}, u32[]{:S(2)}, u32[]{:S(2)}) collective-permute-start(f32[32,5,16,128]{3,2,1,0:T(8,128)S(1)} %get-tuple-element.197), channel_id=1, source_target_pairs={{2,4},{3,5},{4,2},{5,3},{10,12},{11,13},{12,10},{13,11},{18,20},{1... | collective-permute-start | bytes 3932168 | tf_op jit(solution)/shard_map/ppermute | solution.py:415
  81.1 20.6 %collective-permute-start.18 = (f32[16,5,16,128]{3,2,1,0:T(8,128)S(1)}, f32[16,5,16,128]{3,2,1,0:T(8,128)S(1)}, u32[]{:S(2)}, u32[]{:S(2)}) collective-permute-start(f32[16,5,16,128]{3,2,1,0:T(8,128)S(1)} %copy-done.6), channel_id=1, source_target_pairs={{0,2},{1,3},{6,4},{7,5},{8,10},{9,11},{14,12},{15,13},{16,18},{17,... | collective-permute-start | bytes 1966088 | tf_op jit(solution)/shard_map/ppermute | solution.py:339
  86.6 29.3 %collective-permute-start.19 = (f32[16,5,16,128]{3,2,1,0:T(8,128)}, f32[16,5,16,128]{3,2,1,0:T(8,128)S(1)}, u32[]{:S(2)}, u32[]{:S(2)}) collective-permute-start(f32[16,5,16,128]{3,2,1,0:T(8,128)} %collective-permute-done.17.refs_1_), channel_id=1, source_target_pairs={{0,2},{1,3},{6,4},{7,5},{8,10},{9,11},{14,12},{15,13},{16,18},{17,... | collective-permute-start | bytes 1966088 | tf_op jit(solution)/shard_map/ppermute | solution.py:339
  87.9 9.0 %collective-permute-start.6 = (f32[16,5,8,128]{3,2,1,0:T(8,128)S(1)}, f32[16,5,8,128]{3,2,1,0:T(8,128)S(1)}, u32[]{:S(2)}, u32[]{:S(2)}) collective-permute-start(f32[16,5,8,128]{3,2,1,0:T(8,128)S(1)} %get-tuple-element.182), channel_id=1, source_target_pairs={{2,0},{3,1},{4,6},{5,7},{10,8},{11,9},{12,14},{13,15},{18,16},{19,... | collective-permute-start | bytes 983048 | tf_op jit(solution)/shard_map/ppermute | solution.py:339
  89.2 29.9 %collective-permute-start.22 = (f32[16,5,16,128]{3,2,1,0:T(8,128)S(1)}, f32[16,5,16,128]{3,2,1,0:T(8,128)S(1)}, u32[]{:S(2)}, u32[]{:S(2)}) collective-permute-start(f32[16,5,16,128]{3,2,1,0:T(8,128)S(1)} %copy-done.4), channel_id=1, source_target_pairs={{0,1},{1,0},{2,3},{3,2},{4,5},{5,4},{6,7},{7,6},{8,9},{9,8},{10,11... | collective-permute-start | bytes 1966088 | tf_op jit(solution)/shard_map/ppermute | solution.py:347
  96.9 9.2 %collective-permute-start.12 = (f32[8,5,8,128]{3,2,1,0:T(8,128)S(1)}, f32[8,5,8,128]{3,2,1,0:T(8,128)S(1)}, u32[]{:S(2)}, u32[]{:S(2)}) collective-permute-start(f32[8,5,8,128]{3,2,1,0:T(8,128)S(1)} %get-tuple-element.202), channel_id=1, source_target_pairs={{0,1},{1,0},{2,3},{3,2},{4,5},{5,4},{6,7},{7,6},{8,9},{9,8},{10,11... | collective-permute-start | bytes 491528 | tf_op jit(solution)/shard_map/ppermute | solution.py:347
  101.7 28.1 %collective-permute-start.23 = (f32[16,5,16,128]{3,2,1,0:T(8,128)S(1)}, f32[16,5,16,128]{3,2,1,0:T(8,128)S(1)}, u32[]{:S(2)}, u32[]{:S(2)}) collective-permute-start(f32[16,5,16,128]{3,2,1,0:T(8,128)S(1)} %get-tuple-element.237.refs_0_), channel_id=1, source_target_pairs={{0,2},{1,3},{6,4},{7,5},{8,10},{9,11},{14,12},{15,13},{16,18},{17,... | collective-permute-start | bytes 1966088 | tf_op jit(solution)/shard_map/ppermute | solution.py:339
  117.8 12.5 %collective-permute-start.20 = (f32[16,5,16,128]{3,2,1,0:T(8,128)S(1)}, f32[16,5,16,128]{3,2,1,0:T(8,128)S(1)}, u32[]{:S(2)}, u32[]{:S(2)}) collective-permute-start(f32[16,5,16,128]{3,2,1,0:T(8,128)S(1)} %get-tuple-element.225), channel_id=1, source_target_pairs={{2,0},{3,1},{4,6},{5,7},{10,8},{11,9},{12,14},{13,15},{18,16},{19,... | collective-permute-start | bytes 1966088 | tf_op jit(solution)/shard_map/ppermute | solution.py:339
  119.1 18.9 %collective-permute-start.24 = (f32[16,5,16,128]{3,2,1,0:T(8,128)S(1)}, f32[16,5,16,128]{3,2,1,0:T(8,128)S(1)}, u32[]{:S(2)}, u32[]{:S(2)}) collective-permute-start(f32[16,5,16,128]{3,2,1,0:T(8,128)S(1)} %collective-permute-done.22.refs_1_), channel_id=1, source_target_pairs={{0,2},{1,3},{6,4},{7,5},{8,10},{9,11},{14,12},{15,13},{16,18},{17,... | collective-permute-start | bytes 1966088 | tf_op jit(solution)/shard_map/ppermute | solution.py:339
  123.8 26.5 %collective-permute-start.28 = (f32[32,5,16,128]{3,2,1,0:T(8,128)S(1)}, f32[32,5,16,128]{3,2,1,0:T(8,128)S(1)}, u32[]{:S(2)}, u32[]{:S(2)}) collective-permute-start(f32[32,5,16,128]{3,2,1,0:T(8,128)S(1)} %get-tuple-element.220), channel_id=1, source_target_pairs={{2,4},{3,5},{4,2},{5,3},{10,12},{11,13},{12,10},{13,11},{18,20},{1... | collective-permute-start | bytes 3932168 | tf_op jit(solution)/shard_map/ppermute | solution.py:415
  124.5 13.5 %collective-permute-start.30 = (f32[16,5,8,128]{3,2,1,0:T(8,128)S(1)}, f32[16,5,8,128]{3,2,1,0:T(8,128)S(1)}, u32[]{:S(2)}, u32[]{:S(2)}) collective-permute-start(f32[16,5,8,128]{3,2,1,0:T(8,128)S(1)} %copy-done.12), channel_id=1, source_target_pairs={{0,1},{1,0},{2,3},{3,2},{4,5},{5,4},{6,7},{7,6},{8,9},{9,8},{10,11... | collective-permute-start | bytes 983048 | tf_op jit(solution)/shard_map/ppermute | solution.py:347
  129.8 10.2 %collective-permute-start.13 = (f32[4,5,16,128]{3,2,1,0:T(8,128)S(1)}, f32[4,5,16,128]{3,2,1,0:T(8,128)S(1)}, u32[]{:S(2)}, u32[]{:S(2)}) collective-permute-start(f32[4,5,16,128]{3,2,1,0:T(8,128)S(1)} %get-tuple-element.208), channel_id=1, source_target_pairs={{0,8},{8,16},{16,24},{24,0},{1,9},{9,17},{17,25},{25,1},{2,10},{10... | collective-permute-start | bytes 491528 | tf_op jit(solution)/shard_map/ppermute | solution.py:452
  130.3 10.4 %collective-permute-start.14 = (f32[4,5,16,128]{3,2,1,0:T(8,128)S(1)}, f32[4,5,16,128]{3,2,1,0:T(8,128)S(1)}, u32[]{:S(2)}, u32[]{:S(2)}) collective-permute-start(f32[4,5,16,128]{3,2,1,0:T(8,128)S(1)} %get-tuple-element.209), channel_id=1, source_target_pairs={{0,16},{8,24},{16,0},{24,8},{1,17},{9,25},{17,1},{25,9},{2,18},{10... | collective-permute-start | bytes 491528 | tf_op jit(solution)/shard_map/ppermute | solution.py:452
  138.0 9.9 %collective-permute-start.15 = (f32[4,5,16,128]{3,2,1,0:T(8,128)S(1)}, f32[4,5,16,128]{3,2,1,0:T(8,128)S(1)}, u32[]{:S(2)}, u32[]{:S(2)}) collective-permute-start(f32[4,5,16,128]{3,2,1,0:T(8,128)S(1)} %get-tuple-element.210), channel_id=1, source_target_pairs={{0,24},{8,0},{16,8},{24,16},{1,25},{9,1},{17,9},{25,17},{2,26},{10... | collective-permute-start | bytes 491528 | tf_op jit(solution)/shard_map/ppermute | solution.py:452
  138.0 11.3 %collective-permute-start.21 = (f32[8,5,16,128]{3,2,1,0:T(8,128)S(1)}, f32[8,5,16,128]{3,2,1,0:T(8,128)S(1)}, u32[]{:S(2)}, u32[]{:S(2)}) collective-permute-start(f32[8,5,16,128]{3,2,1,0:T(8,128)S(1)} %get-tuple-element.230), channel_id=1, source_target_pairs={{0,1},{1,0},{2,3},{3,2},{4,5},{5,4},{6,7},{7,6},{8,9},{9,8},{10,11... | collective-permute-start | bytes 983048 | tf_op jit(solution)/shard_map/ppermute | solution.py:347
  140.0 38.0 %collective-permute-start.37 = (f32[32,5,16,128]{3,2,1,0:T(8,128)S(1)}, f32[32,5,16,128]{3,2,1,0:T(8,128)S(1)}, u32[]{:S(2)}, u32[]{:S(2)}) collective-permute-start(f32[32,5,16,128]{3,2,1,0:T(8,128)S(1)} %get-tuple-element.241), channel_id=1, source_target_pairs={{2,4},{3,5},{4,2},{5,3},{10,12},{11,13},{12,10},{13,11},{18,20},{1... | collective-permute-start | bytes 3932168 | tf_op jit(solution)/shard_map/ppermute | solution.py:415
  140.7 15.3 %collective-permute-start.32 = (f32[16,5,8,128]{3,2,1,0:T(8,128)S(1)}, f32[16,5,8,128]{3,2,1,0:T(8,128)S(1)}, u32[]{:S(2)}, u32[]{:S(2)}) collective-permute-start(f32[16,5,8,128]{3,2,1,0:T(8,128)S(1)} %collective-permute-done.30.refs_1_), channel_id=1, source_target_pairs={{0,2},{1,3},{6,4},{7,5},{8,10},{9,11},{14,12},{15,13},{16,18},{17,... | collective-permute-start | bytes 983048 | tf_op jit(solution)/shard_map/ppermute | solution.py:339
  148.0 14.0 %collective-permute-start.31 = (f32[16,5,8,128]{3,2,1,0:T(8,128)S(1)}, f32[16,5,8,128]{3,2,1,0:T(8,128)S(1)}, u32[]{:S(2)}, u32[]{:S(2)}) collective-permute-start(f32[16,5,8,128]{3,2,1,0:T(8,128)S(1)} %copy-done.10), channel_id=1, source_target_pairs={{0,2},{1,3},{6,4},{7,5},{8,10},{9,11},{14,12},{15,13},{16,18},{17,... | collective-permute-start | bytes 983048 | tf_op jit(solution)/shard_map/ppermute | solution.py:339
  150.4 18.1 %collective-permute-start.29 = (f32[16,5,16,128]{3,2,1,0:T(8,128)S(1)}, f32[16,5,16,128]{3,2,1,0:T(8,128)S(1)}, u32[]{:S(2)}, u32[]{:S(2)}) collective-permute-start(f32[16,5,16,128]{3,2,1,0:T(8,128)S(1)} %get-tuple-element.253), channel_id=1, source_target_pairs={{2,0},{3,1},{4,6},{5,7},{10,8},{11,9},{12,14},{13,15},{18,16},{19,... | collective-permute-start | bytes 1966088 | tf_op jit(solution)/shard_map/ppermute | solution.py:339
  151.7 18.4 %collective-permute-start.25 = (f32[4,5,32,128]{3,2,1,0:T(8,128)S(1)}, f32[4,5,32,128]{3,2,1,0:T(8,128)S(1)}, u32[]{:S(2)}, u32[]{:S(2)}) collective-permute-start(f32[4,5,32,128]{3,2,1,0:T(8,128)S(1)} %get-tuple-element.245), channel_id=1, source_target_pairs={{0,8},{8,16},{16,24},{24,0},{1,9},{9,17},{17,25},{25,1},{2,10},{10... | collective-permute-start | bytes 983048 | tf_op jit(solution)/shard_map/ppermute | solution.py:452
  156.0 14.8 %collective-permute-start.26 = (f32[4,5,32,128]{3,2,1,0:T(8,128)S(1)}, f32[4,5,32,128]{3,2,1,0:T(8,128)S(1)}, u32[]{:S(2)}, u32[]{:S(2)}) collective-permute-start(f32[4,5,32,128]{3,2,1,0:T(8,128)S(1)} %get-tuple-element.246), channel_id=1, source_target_pairs={{0,16},{8,24},{16,0},{24,8},{1,17},{9,25},{17,1},{25,9},{2,18},{10... | collective-permute-start | bytes 983048 | tf_op jit(solution)/shard_map/ppermute | solution.py:452
  162.0 8.9 %collective-permute-start.27 = (f32[4,5,32,128]{3,2,1,0:T(8,128)S(1)}, f32[4,5,32,128]{3,2,1,0:T(8,128)S(1)}, u32[]{:S(2)}, u32[]{:S(2)}) collective-permute-start(f32[4,5,32,128]{3,2,1,0:T(8,128)S(1)} %get-tuple-element.247), channel_id=1, source_target_pairs={{0,24},{8,0},{16,8},{24,16},{1,25},{9,1},{17,9},{25,17},{2,26},{10... | collective-permute-start | bytes 983048 | tf_op jit(solution)/shard_map/ppermute | solution.py:452
  168.6 8.4 %collective-permute-start.33 = (f32[8,5,16,128]{3,2,1,0:T(8,128)S(1)}, f32[8,5,16,128]{3,2,1,0:T(8,128)S(1)}, u32[]{:S(2)}, u32[]{:S(2)}) collective-permute-start(f32[8,5,16,128]{3,2,1,0:T(8,128)S(1)} %get-tuple-element.265), channel_id=1, source_target_pairs={{0,1},{1,0},{2,3},{3,2},{4,5},{5,4},{6,7},{7,6},{8,9},{9,8},{10,11... | collective-permute-start | bytes 983048 | tf_op jit(solution)/shard_map/ppermute | solution.py:347
  170.2 10.9 %collective-permute-start.39 = (f32[32,5,8,128]{3,2,1,0:T(8,128)S(1)}, f32[32,5,8,128]{3,2,1,0:T(8,128)S(1)}, u32[]{:S(2)}, u32[]{:S(2)}) collective-permute-start(f32[32,5,8,128]{3,2,1,0:T(8,128)S(1)} %get-tuple-element.260), channel_id=1, source_target_pairs={{2,4},{3,5},{4,2},{5,3},{10,12},{11,13},{12,10},{13,11},{18,20},{1... | collective-permute-start | bytes 1966088 | tf_op jit(solution)/shard_map/ppermute | solution.py:415
  178.1 19.6 %collective-permute-start.38 = (f32[16,5,16,128]{3,2,1,0:T(8,128)S(1)}, f32[16,5,16,128]{3,2,1,0:T(8,128)S(1)}, u32[]{:S(2)}, u32[]{:S(2)}) collective-permute-start(f32[16,5,16,128]{3,2,1,0:T(8,128)S(1)} %get-tuple-element.279), channel_id=1, source_target_pairs={{2,0},{3,1},{4,6},{5,7},{10,8},{11,9},{12,14},{13,15},{18,16},{19,... | collective-permute-start | bytes 1966088 | tf_op jit(solution)/shard_map/ppermute | solution.py:339
  179.4 22.1 %collective-permute-start.34 = (f32[4,5,32,128]{3,2,1,0:T(8,128)S(1)}, f32[4,5,32,128]{3,2,1,0:T(8,128)S(1)}, u32[]{:S(2)}, u32[]{:S(2)}) collective-permute-start(f32[4,5,32,128]{3,2,1,0:T(8,128)S(1)} %get-tuple-element.271), channel_id=1, source_target_pairs={{0,8},{8,16},{16,24},{24,0},{1,9},{9,17},{17,25},{25,1},{2,10},{10... | collective-permute-start | bytes 983048 | tf_op jit(solution)/shard_map/ppermute | solution.py:452
  179.5 22.0 %collective-permute-start.35 = (f32[4,5,32,128]{3,2,1,0:T(8,128)S(1)}, f32[4,5,32,128]{3,2,1,0:T(8,128)S(1)}, u32[]{:S(2)}, u32[]{:S(2)}) collective-permute-start(f32[4,5,32,128]{3,2,1,0:T(8,128)S(1)} %get-tuple-element.272), channel_id=1, source_target_pairs={{0,16},{8,24},{16,0},{24,8},{1,17},{9,25},{17,1},{25,9},{2,18},{10... | collective-permute-start | bytes 983048 | tf_op jit(solution)/shard_map/ppermute | solution.py:452
  181.1 20.3 %collective-permute-start.41 = (f32[16,5,8,128]{3,2,1,0:T(8,128)S(1)}, f32[16,5,8,128]{3,2,1,0:T(8,128)S(1)}, u32[]{:S(2)}, u32[]{:S(2)}) collective-permute-start(f32[16,5,8,128]{3,2,1,0:T(8,128)S(1)} %get-tuple-element.283), channel_id=1, source_target_pairs={{2,0},{3,1},{4,6},{5,7},{10,8},{11,9},{12,14},{13,15},{18,16},{19,... | collective-permute-start | bytes 983048 | tf_op jit(solution)/shard_map/ppermute | solution.py:339
  182.4 19.1 %collective-permute-start.36 = (f32[4,5,32,128]{3,2,1,0:T(8,128)S(1)}, f32[4,5,32,128]{3,2,1,0:T(8,128)S(1)}, u32[]{:S(2)}, u32[]{:S(2)}) collective-permute-start(f32[4,5,32,128]{3,2,1,0:T(8,128)S(1)} %get-tuple-element.273), channel_id=1, source_target_pairs={{0,24},{8,0},{16,8},{24,16},{1,25},{9,1},{17,9},{25,17},{2,26},{10... | collective-permute-start | bytes 983048 | tf_op jit(solution)/shard_map/ppermute | solution.py:452
  197.7 7.1 %collective-permute-start.40 = (f32[8,5,16,128]{3,2,1,0:T(8,128)S(1)}, f32[8,5,16,128]{3,2,1,0:T(8,128)S(1)}, u32[]{:S(2)}, u32[]{:S(2)}) collective-permute-start(f32[8,5,16,128]{3,2,1,0:T(8,128)S(1)} %get-tuple-element.288), channel_id=1, source_target_pairs={{0,1},{1,0},{2,3},{3,2},{4,5},{5,4},{6,7},{7,6},{8,9},{9,8},{10,11... | collective-permute-start | bytes 983048 | tf_op jit(solution)/shard_map/ppermute | solution.py:347
  205.8 9.5 %collective-permute-start.42 = (f32[4,5,32,128]{3,2,1,0:T(8,128)S(1)}, f32[4,5,32,128]{3,2,1,0:T(8,128)S(1)}, u32[]{:S(2)}, u32[]{:S(2)}) collective-permute-start(f32[4,5,32,128]{3,2,1,0:T(8,128)S(1)} %get-tuple-element.300), channel_id=1, source_target_pairs={{0,8},{8,16},{16,24},{24,0},{1,9},{9,17},{17,25},{25,1},{2,10},{10... | collective-permute-start | bytes 983048 | tf_op jit(solution)/shard_map/ppermute | solution.py:452
  205.9 10.6 %collective-permute-start.43 = (f32[4,5,32,128]{3,2,1,0:T(8,128)S(1)}, f32[4,5,32,128]{3,2,1,0:T(8,128)S(1)}, u32[]{:S(2)}, u32[]{:S(2)}) collective-permute-start(f32[4,5,32,128]{3,2,1,0:T(8,128)S(1)} %get-tuple-element.301), channel_id=1, source_target_pairs={{0,16},{8,24},{16,0},{24,8},{1,17},{9,25},{17,1},{25,9},{2,18},{10... | collective-permute-start | bytes 983048 | tf_op jit(solution)/shard_map/ppermute | solution.py:452
  207.5 14.5 %collective-permute-start.44 = (f32[4,5,32,128]{3,2,1,0:T(8,128)S(1)}, f32[4,5,32,128]{3,2,1,0:T(8,128)S(1)}, u32[]{:S(2)}, u32[]{:S(2)}) collective-permute-start(f32[4,5,32,128]{3,2,1,0:T(8,128)S(1)} %get-tuple-element.302), channel_id=1, source_target_pairs={{0,24},{8,0},{16,8},{24,16},{1,25},{9,1},{17,9},{25,17},{2,26},{10... | collective-permute-start | bytes 983048 | tf_op jit(solution)/shard_map/ppermute | solution.py:452
  208.8 5.3 %collective-permute-start.45 = (f32[8,5,8,128]{3,2,1,0:T(8,128)S(1)}, f32[8,5,8,128]{3,2,1,0:T(8,128)S(1)}, u32[]{:S(2)}, u32[]{:S(2)}) collective-permute-start(f32[8,5,8,128]{3,2,1,0:T(8,128)S(1)} %get-tuple-element.303), channel_id=1, source_target_pairs={{0,1},{1,0},{2,3},{3,2},{4,5},{5,4},{6,7},{7,6},{8,9},{9,8},{10,11... | collective-permute-start | bytes 491528 | tf_op jit(solution)/shard_map/ppermute | solution.py:347
  222.8 5.5 %collective-permute-start.46 = (f32[4,5,16,128]{3,2,1,0:T(8,128)S(1)}, f32[4,5,16,128]{3,2,1,0:T(8,128)S(1)}, u32[]{:S(2)}, u32[]{:S(2)}) collective-permute-start(f32[4,5,16,128]{3,2,1,0:T(8,128)S(1)} %get-tuple-element.325), channel_id=1, source_target_pairs={{0,8},{8,16},{16,24},{24,0},{1,9},{9,17},{17,25},{25,1},{2,10},{10... | collective-permute-start | bytes 491528 | tf_op jit(solution)/shard_map/ppermute | solution.py:452
  223.6 7.1 %collective-permute-start.47 = (f32[4,5,16,128]{3,2,1,0:T(8,128)S(1)}, f32[4,5,16,128]{3,2,1,0:T(8,128)S(1)}, u32[]{:S(2)}, u32[]{:S(2)}) collective-permute-start(f32[4,5,16,128]{3,2,1,0:T(8,128)S(1)} %get-tuple-element.326), channel_id=1, source_target_pairs={{0,16},{8,24},{16,0},{24,8},{1,17},{9,25},{17,1},{25,9},{2,18},{10... | collective-permute-start | bytes 491528 | tf_op jit(solution)/shard_map/ppermute | solution.py:452
  225.1 5.9 %collective-permute-start.48 = (f32[4,5,16,128]{3,2,1,0:T(8,128)S(1)}, f32[4,5,16,128]{3,2,1,0:T(8,128)S(1)}, u32[]{:S(2)}, u32[]{:S(2)}) collective-permute-start(f32[4,5,16,128]{3,2,1,0:T(8,128)S(1)} %get-tuple-element.327), channel_id=1, source_target_pairs={{0,24},{8,0},{16,8},{24,16},{1,25},{9,1},{17,9},{25,17},{2,26},{10... | collective-permute-start | bytes 491528 | tf_op jit(solution)/shard_map/ppermute | solution.py:452
  (24 other events, 183.9 us)
where the time goes:
time: 236 us; the launch traced here: 234 us
  waiting for transfers between devices  103 us (44%)
  starting transfers between devices  87.1 us (37%)
  Pallas kernels  26 us (11%)
  local copies, waits for them, and re-layouts  11.5 us (5%)
  other arithmetic  4.77 us (2%)
    ppermute x16, waiting for transfers between devices, hop(): return lax.ppermute(array, 'member', pairs)  69.5 us
    ppermute x16, starting transfers between devices, hop(): return lax.ppermute(array, 'member', pairs)  56.5 us
    ppermute x11, waiting for transfers between devices, hop_x(): return lax.ppermute(array, 'member', pairs)  18.1 us
    pallas_call x20, Pallas kernels, whole(): pl.pallas_call(kernel, out_shape=out_shapes, in_specs=[pl.BlockSpec(memor...  13.5 us
    ppermute x11, starting transfers between devices, hop_x(): return lax.ppermute(array, 'member', pairs)  13.2 us
    ppermute x15, starting transfers between devices, second(): received.append(lax.ppermute(share, 'group', around) if way > 0 else share)  11.6 us
    ppermute x15, waiting for transfers between devices, second(): received.append(lax.ppermute(share, 'group', around) if way > 0 else share)  10.6 us
    unnamed x46, local copies, waits for them, and re-layouts  9.94 us
  transfers between devices with their start and end apart: 49, of which 25 were waited for; matrix products, arithmetic and copies ran while one was open for 2% of the time, Pallas kernels for 6%

commit v1 on v0

--- a/solution.py
+++ b/solution.py
@@ -286,14 +286,20 @@
     )(place, prolong_two, *pieces)
 
 
-def sweep(fine_blocks, neighbours, diag_inverse, right_side, initial_guess):
+def around(initial_guess):
+    axes = ("group", "member")
+    devices = lax.axis_size(axes)
+    before = lax.ppermute(initial_guess, axes, [(i, (i + 1) % devices) for i in range(devices)])
+    after = lax.ppermute(initial_guess, axes, [(i, (i - 1) % devices) for i in range(devices)])
+    return [before, initial_guess, after]
+
+
+def sweep(fine_blocks, neighbours, diag_inverse, right_side, initial_guess, window):
     rows = fine_blocks.shape[0]
     axes = ("group", "member")
     devices = lax.axis_size(axes)
     device = lax.axis_index(axes)
-    before = lax.ppermute(initial_guess, axes, [(i, (i + 1) % devices) for i in range(devices)])
-    after = lax.ppermute(initial_guess, axes, [(i, (i - 1) % devices) for i in range(devices)])
-    window = jnp.concatenate([before, initial_guess, after], axis=0)
+    window = jnp.concatenate(window, axis=0)
     position = (neighbours - device * rows + rows) % (rows * devices)
     nearby = window[position]
     product = jnp.sum(fine_blocks * nearby[:, :, None, :], axis=(1, 3))
@@ -355,7 +361,7 @@
         return arrays + [hop(array, d, 0, 0) for d in range(1, half) for array in arrays]
 
     tags = jnp.stack(along([pair_one] * x_count))
-    slot_one, tags = lax.optimization_barrier((slot_one, tags))
+    slot_one, tags, window = lax.optimization_barrier((slot_one, tags, around(initial_guess)))
     owner_rows = jnp.concatenate([tags] + [hop(tags, d, 0, 0) for d in range(1, half)])
     owner = owner_rows // rows_one % members
     owner_z, owner_x = owner // x_count, owner % x_count
@@ -400,7 +406,7 @@
         held = coming[chunk]
         if chunk == min(1, len(steps) - 1):
             later, before[0] = lax.optimization_barrier((neighbours, before[0]))
-            swept = sweep(fine_blocks, later, diag_inverse, right_side, initial_guess)
+            swept = sweep(fine_blocks, later, diag_inverse, right_side, initial_guess, window)
             held, swept = lax.optimization_barrier((held, swept))
             smoothed.append(swept)
         total = half * x_count * rows_one
@@ -437,7 +443,8 @@
         )
 
     def second(chunk, ours):
-        received[-groups:], ours = lax.optimization_barrier((received[-groups:], ours))
+        if chunk + 1 < len(steps):
+            received[-groups:], ours = lax.optimization_barrier((received[-groups:], ours))
         height = x_count * steps[chunk]
         shares = in_turn(
             functools.partial(second_kernel, x_count),
@@ -448,8 +455,8 @@
             scratch=[pltpu.VMEM((groups * rows_two, links, height, size), jnp.float32)],
         )
         for way, share in enumerate(shares):
-            around = [(g, (g + way) % groups) for g in range(groups)]
-            received.append(lax.ppermute(share, "group", around) if way > 0 else share)
+            circle = [(g, (g + way) % groups) for g in range(groups)]
+            received.append(lax.ppermute(share, "group", circle) if way > 0 else share)
         return ours
 
     stages, shares = (combine, finish, settle, second), (1.0, 0.5, 0.25)

time: 236 us -> 238 us (level)
  waiting for transfers between devices: 103 us -> 110 us
  starting transfers between devices: 87.1 us -> 83.3 us
    ppermute x16, starting transfers between devices: 56.5 us -> 51.6 us  [hop(): return lax.ppermute(array, 'member', pairs)]
    ppermute x11, waiting for transfers between devices: 18.1 us -> 22.1 us  [hop_x(): return lax.ppermute(array, 'member', pairs)]
    ppermute x11, starting transfers between devices: 13.2 us -> 16 us  [hop_x(): return lax.ppermute(array, 'member', pairs)]
    ppermute x16, waiting for transfers between devices: 69.5 us -> 72.3 us  [hop(): return lax.ppermute(array, 'member', pairs)]
    unnamed x46 -> x40, local copies, waits for them, and re-layouts: 9.94 us -> 9.07 us
  transfers between devices with their start and end apart: 49 -> 49, of which waited for: 25 -> 23; matrix products, arithmetic and copies ran while one was open for 2% -> 2% of each run, Pallas kernels for 6% -> 7%
where the time goes in v1:
time: 238 us; the launch traced here: 236 us
  waiting for transfers between devices  110 us (46%)
  starting transfers between devices  83.3 us (35%)
  Pallas kernels  26.3 us (11%)
  local copies, waits for them, and re-layouts  10.6 us (4%)
  other arithmetic  4.73 us (2%)
    ppermute x16, waiting for transfers between devices, hop(): return lax.ppermute(array, 'member', pairs)  72.3 us
    ppermute x16, starting transfers between devices, hop(): return lax.ppermute(array, 'member', pairs)  51.6 us
    ppermute x11, waiting for transfers between devices, hop_x(): return lax.ppermute(array, 'member', pairs)  22.1 us
    ppermute x11, starting transfers between devices, hop_x(): return lax.ppermute(array, 'member', pairs)  16 us
    ppermute x15, waiting for transfers between devices, second(): received.append(lax.ppermute(share, 'group', circle) if way > 0 else share)  15.7 us
    pallas_call x20, Pallas kernels, whole(): pl.pallas_call(kernel, out_shape=out_shapes, in_specs=[pl.BlockSpec(memor...  13.8 us
    unnamed x40, local copies, waits for them, and re-layouts  9.07 us
    pallas_call x1, Pallas kernels, prepare(): pl.pallas_call(functools.partial(prepare_kernel, x_count), out_shape=[jax...  6.75 us
  transfers between devices with their start and end apart: 49, of which 23 were waited for; matrix products, arithmetic and copies ran while one was open for 2% of the time, Pallas kernels for 7%

profile of v1, /device:TPU:0, one launch (start us, length us, event | category | flops | bytes accessed | tf_op | source)
XLA Modules:
  0.0 236.2 jit_solution(937774232878955722)
XLA Ops:
  0.6 3.0 %collective-permute-start.1 = (f32[16,128]{1,0:T(8,128)}, f32[16,128]{1,0:T(8,128)S(1)}, u32[]{:S(2)}, u32[]{:S(2)}) collective-permute-start(f32[16,128]{1,0:T(8,128)} %param.21), channel_id=1, source_target_pairs={{0,1},{1,2},{2,3},{3,4},{4,5},{5,6},{6,7},{7,8},{8,9},{9,10},{10,1... | collective-permute-start | bytes 24584 | tf_op jit(solution)/shard_map/ppermute | solution.py:292
  3.6 3.5 %collective-permute-start.2 = (f32[16,128]{1,0:T(8,128)}, f32[16,128]{1,0:T(8,128)S(1)}, u32[]{:S(2)}, u32[]{:S(2)}) collective-permute-start(f32[16,128]{1,0:T(8,128)} %param.21), channel_id=1, source_target_pairs={{0,31},{1,0},{2,1},{3,2},{4,3},{5,4},{6,5},{7,6},{8,7},{9,8},{10,9... | collective-permute-start | bytes 24584 | tf_op jit(solution)/shard_map/ppermute | solution.py:293
  7.1 3.7 %collective-permute-done = s32[16]{0:T(128)S(1)} collective-permute-done((s32[16]{0:T(128)}, s32[16]{0:T(128)S(1)}, u32[]{:S(2)}, u32[]{:S(2)}) %collective-permute-start) | collective-permute-done | bytes 96 | tf_op jit(solution)/shard_map/ppermute | solution.py:353
  12.3 2.5 %copy-done = f32[16,5,128,128]{3,2,1,0:T(8,128)S(1)} copy-done((f32[16,5,128,128]{3,2,1,0:T(8,128)S(1)}, f32[16,5,128,128]{3,2,1,0:T(8,128)}, u32[]{:S(2)}) %copy-start) | copy-done | bytes 5242904
  15.6 6.8 %prepare.1 = (f32[16,5,8,128]{3,2,1,0:T(8,128)S(1)}, f32[16,5,16,128]{3,2,1,0:T(8,128)}, f32[16,5,16,128]{3,2,1,0:T(8,128)S(1)}, f32[16,5,16,128]{3,2,1,0:T(8,12...) custom-call(s32[16,5]{1,0:T(8,128)S(1)} %copy.16.slot_ref, ...), custom_call_target="tpu_custom_call" | custom-call | flops 2684354560 | bytes 10485760 | tf_op jit(solution)/shard_map/prepare/pallas_call | solution.py:96
  25.6 2.0 collective-permute-start.5
  27.6 6.1 %collective-permute-done.4.refs_1_ = f32[16,5,8,128]{3,2,1,0:T(8,128)S(1)} collective-permute-done((f32[16,5,8,128]{3,2,1,0:T(8,128)S(1)}, f32[16,5,8,128]{3,2,1,0:T(8,128)S(1)}, u32[]{:S(2)}, u32[]{:S(2)}) %collective-permute-start.4) | collective-permute-done | bytes 327712 | tf_op jit(solution)/shard_map/ppermute | solution.py:353
  33.8 1.3 collective-permute-start.6
  37.1 3.2 %collective-permute-done.3 = s32[2,16]{1,0:T(2,128)S(1)} collective-permute-done((s32[2,16]{1,0:T(2,128)S(1)}, s32[2,16]{1,0:T(2,128)S(1)}, u32[]{:S(2)}, u32[]{:S(2)}) %collective-permute-start.3) | collective-permute-done | bytes 160 | tf_op jit(solution)/shard_map/ppermute | solution.py:345
  40.3 5.2 %collective-permute-start.10 = (f32[16,5,16,128]{3,2,1,0:T(8,128)}, f32[16,5,16,128]{3,2,1,0:T(8,128)}, u32[]{:S(2)}, u32[]{:S(2)}) collective-permute-start(f32[16,5,16,128]{3,2,1,0:T(8,128)} %get-tuple-element.193.refs_0_), channel_id=1, source_target_pairs={{0,2},{1,3},{6,4},{7,5},{8,10},{9,11},{14,12},{15,13},{16,18},{17,... | collective-permute-start | bytes 1966088 | tf_op jit(solution)/shard_map/ppermute | solution.py:345
  47.3 1.9 combine.5
  50.1 1.4 collective-permute-start.17
  51.8 6.6 %collective-permute-start.11 = (f32[16,5,16,128]{3,2,1,0:T(8,128)}, f32[16,5,16,128]{3,2,1,0:T(8,128)}, u32[]{:S(2)}, u32[]{:S(2)}) collective-permute-start(f32[16,5,16,128]{3,2,1,0:T(8,128)} %collective-permute-done.9.refs_1_), channel_id=1, source_target_pairs={{0,2},{1,3},{6,4},{7,5},{8,10},{9,11},{14,12},{15,13},{16,18},{17,... | collective-permute-start | bytes 1966088 | tf_op jit(solution)/shard_map/ppermute | solution.py:345
  60.0 3.0 %multiply_reduce_fusion = f32[16,128]{1,0:T(8,128)S(1)} fusion(f32[16,5,128,128]{3,2,1,0:T(8,128)} %fine_ref.1, f32[16,5,128]{2,1,0:T(8,128)S(1)} %reshape.12), kind=kLoop, calls=%fused_computation.1 | loop fusion | flops 2619392 | bytes 5292032 | tf_op jit(solution)/shard_map/reduce_sum | solution.py:305
  64.0 7.4 %collective-permute-done.11.refs_3_ = f32[16,5,16,128]{3,2,1,0:T(8,128)} collective-permute-done((f32[16,5,16,128]{3,2,1,0:T(8,128)}, f32[16,5,16,128]{3,2,1,0:T(8,128)}, u32[]{:S(2)}, u32[]{:S(2)}) %collective-permute-start.11) | collective-permute-done | bytes 655392 | tf_op jit(solution)/shard_map/ppermute | solution.py:345
  71.4 2.4 %combine.6 = (f32[32,5,16,128]{3,2,1,0:T(8,128)S(1)}, f32[64,5,16,128]{3,2,1,0:T(8,128)S(1)}) custom-call(s32[4,16]{1,0:T(4,128)S(1)} %fusion.7.target_ref, f32[16,5,16,128]{3,2,1,0:T(8,128)} %get-tuple-element.193.refs_0_, f32[16,5,16,128]{3,2,1,0:T(8,128)} %collective-permute-done.9.refs_1_, f32[16,5,16,128]{3,2,1,0:T(8,128)} %collective-permute-done.10.refs_2_, ...), custom_call_target="tpu_custom_call" | custom-call | flops 6000000000 | tf_op jit(solution)/shard_map/combine/pallas_call | solution.py:130
  74.6 11.3 %collective-permute-start.18 = (f32[16,5,16,128]{3,2,1,0:T(8,128)S(1)}, f32[16,5,16,128]{3,2,1,0:T(8,128)S(1)}, u32[]{:S(2)}, u32[]{:S(2)}) collective-permute-start(f32[16,5,16,128]{3,2,1,0:T(8,128)S(1)} %copy-done.6), channel_id=1, source_target_pairs={{0,2},{1,3},{6,4},{7,5},{8,10},{9,11},{14,12},{15,13},{16,18},{17,... | collective-permute-start | bytes 1966088 | tf_op jit(solution)/shard_map/ppermute | solution.py:345
  85.9 1.3 collective-permute-start.19
  88.6 1.8 collective-permute-start.22
  90.4 6.2 %collective-permute-done.8.refs_2_ = f32[16,5,8,128]{3,2,1,0:T(8,128)S(1)} collective-permute-done((f32[16,5,8,128]{3,2,1,0:T(8,128)S(1)}, f32[16,5,8,128]{3,2,1,0:T(8,128)S(1)}, u32[]{:S(2)}, u32[]{:S(2)}) %collective-permute-start.8) | collective-permute-done | bytes 327712 | tf_op jit(solution)/shard_map/ppermute | solution.py:345
  96.6 2.7 %collective-permute-start.12 = (f32[8,5,8,128]{3,2,1,0:T(8,128)S(1)}, f32[8,5,8,128]{3,2,1,0:T(8,128)S(1)}, u32[]{:S(2)}, u32[]{:S(2)}) collective-permute-start(f32[8,5,8,128]{3,2,1,0:T(8,128)S(1)} %get-tuple-element.202), channel_id=1, source_target_pairs={{0,1},{1,0},{2,3},{3,2},{4,5},{5,4},{6,7},{7,6},{8,9},{9,8},{10,11... | collective-permute-start | bytes 491528 | tf_op jit(solution)/shard_map/ppermute | solution.py:353
  99.3 1.7 collective-permute-done.18.refs_2_
  101.0 4.4 %collective-permute-start.23 = (f32[16,5,16,128]{3,2,1,0:T(8,128)S(1)}, f32[16,5,16,128]{3,2,1,0:T(8,128)S(1)}, u32[]{:S(2)}, u32[]{:S(2)}) collective-permute-start(f32[16,5,16,128]{3,2,1,0:T(8,128)S(1)} %get-tuple-element.237.refs_0_), channel_id=1, source_target_pairs={{0,2},{1,3},{6,4},{7,5},{8,10},{9,11},{14,12},{15,13},{16,18},{17,... | collective-permute-start | bytes 1966088 | tf_op jit(solution)/shard_map/ppermute | solution.py:345
  105.4 2.0 collective-permute-done.12.refs_1_.refs_5_
  108.3 6.8 %collective-permute-done.19.refs_3_ = f32[16,5,16,128]{3,2,1,0:T(8,128)S(1)} collective-permute-done((f32[16,5,16,128]{3,2,1,0:T(8,128)}, f32[16,5,16,128]{3,2,1,0:T(8,128)S(1)}, u32[]{:S(2)}, u32[]{:S(2)}) %collective-permute-start.19) | collective-permute-done | bytes 655392 | tf_op jit(solution)/shard_map/ppermute | solution.py:345
  115.2 1.8 combine.7
  117.1 1.3 collective-permute-start.20
  118.4 4.6 %collective-permute-start.24 = (f32[16,5,16,128]{3,2,1,0:T(8,128)S(1)}, f32[16,5,16,128]{3,2,1,0:T(8,128)S(1)}, u32[]{:S(2)}, u32[]{:S(2)}) collective-permute-start(f32[16,5,16,128]{3,2,1,0:T(8,128)S(1)} %collective-permute-done.22.refs_1_), channel_id=1, source_target_pairs={{0,2},{1,3},{6,4},{7,5},{8,10},{9,11},{14,12},{15,13},{16,18},{17,... | collective-permute-start | bytes 1966088 | tf_op jit(solution)/shard_map/ppermute | solution.py:345
  123.8 1.8 collective-permute-start.30
  125.7 3.4 %collective-permute-done.23.refs_2_ = f32[16,5,16,128]{3,2,1,0:T(8,128)S(1)} collective-permute-done((f32[16,5,16,128]{3,2,1,0:T(8,128)S(1)}, f32[16,5,16,128]{3,2,1,0:T(8,128)S(1)}, u32[]{:S(2)}, u32[]{:S(2)}) %collective-permute-start.23) | collective-permute-done | bytes 655392 | tf_op jit(solution)/shard_map/ppermute | solution.py:345
  129.9 10.3 %collective-permute-done.24.refs_3_ = f32[16,5,16,128]{3,2,1,0:T(8,128)S(1)} collective-permute-done((f32[16,5,16,128]{3,2,1,0:T(8,128)S(1)}, f32[16,5,16,128]{3,2,1,0:T(8,128)S(1)}, u32[]{:S(2)}, u32[]{:S(2)}) %collective-permute-start.24) | collective-permute-done | bytes 655392 | tf_op jit(solution)/shard_map/ppermute | solution.py:345
  140.2 2.6 %collective-permute-start.21 = (f32[8,5,16,128]{3,2,1,0:T(8,128)S(1)}, f32[8,5,16,128]{3,2,1,0:T(8,128)S(1)}, u32[]{:S(2)}, u32[]{:S(2)}) collective-permute-start(f32[8,5,16,128]{3,2,1,0:T(8,128)S(1)} %get-tuple-element.230), channel_id=1, source_target_pairs={{0,1},{1,0},{2,3},{3,2},{4,5},{5,4},{6,7},{7,6},{8,9},{9,8},{10,11... | collective-permute-start | bytes 983048 | tf_op jit(solution)/shard_map/ppermute | solution.py:353
  144.9 5.8 %collective-permute-start.32 = (f32[16,5,8,128]{3,2,1,0:T(8,128)S(1)}, f32[16,5,8,128]{3,2,1,0:T(8,128)S(1)}, u32[]{:S(2)}, u32[]{:S(2)}) collective-permute-start(f32[16,5,8,128]{3,2,1,0:T(8,128)S(1)} %collective-permute-done.30.refs_1_), channel_id=1, source_target_pairs={{0,2},{1,3},{6,4},{7,5},{8,10},{9,11},{14,12},{15,13},{16,18},{17,... | collective-permute-start | bytes 983048 | tf_op jit(solution)/shard_map/ppermute | solution.py:345
  150.7 1.3 collective-permute-start.31
  154.5 4.3 %collective-permute-done.32.refs_3_ = f32[16,5,8,128]{3,2,1,0:T(8,128)S(1)} collective-permute-done((f32[16,5,8,128]{3,2,1,0:T(8,128)S(1)}, f32[16,5,8,128]{3,2,1,0:T(8,128)S(1)}, u32[]{:S(2)}, u32[]{:S(2)}) %collective-permute-start.32) | collective-permute-done | bytes 327712 | tf_op jit(solution)/shard_map/ppermute | solution.py:345
  158.8 6.0 %collective-permute-done.31.refs_2_ = f32[16,5,8,128]{3,2,1,0:T(8,128)S(1)} collective-permute-done((f32[16,5,8,128]{3,2,1,0:T(8,128)S(1)}, f32[16,5,8,128]{3,2,1,0:T(8,128)S(1)}, u32[]{:S(2)}, u32[]{:S(2)}) %collective-permute-start.31) | collective-permute-done | bytes 327712 | tf_op jit(solution)/shard_map/ppermute | solution.py:345
  165.8 5.5 %collective-permute-done.29.refs_2_ = f32[16,5,16,128]{3,2,1,0:T(8,128)S(1)} collective-permute-done((f32[16,5,16,128]{3,2,1,0:T(8,128)S(1)}, f32[16,5,16,128]{3,2,1,0:T(8,128)S(1)}, u32[]{:S(2)}, u32[]{:S(2)}) %collective-permute-start.29) | collective-permute-done | bytes 655392 | tf_op jit(solution)/shard_map/ppermute | solution.py:345
  173.3 6.5 %collective-permute-done.33.refs_1_.refs_7_ = f32[8,5,16,128]{3,2,1,0:T(8,128)S(1)} collective-permute-done((f32[8,5,16,128]{3,2,1,0:T(8,128)S(1)}, f32[8,5,16,128]{3,2,1,0:T(8,128)S(1)}, u32[]{:S(2)}, u32[]{:S(2)}) %collective-permute-start.33) | collective-permute-done | bytes 327712 | tf_op jit(solution)/shard_map/ppermute | solution.py:353
  183.8 1.7 collective-permute-start.36
  185.5 14.1 %collective-permute-done.38.refs_2_ = f32[16,5,16,128]{3,2,1,0:T(8,128)S(1)} collective-permute-done((f32[16,5,16,128]{3,2,1,0:T(8,128)S(1)}, f32[16,5,16,128]{3,2,1,0:T(8,128)S(1)}, u32[]{:S(2)}, u32[]{:S(2)}) %collective-permute-start.38) | collective-permute-done | bytes 655392 | tf_op jit(solution)/shard_map/ppermute | solution.py:345
  199.7 2.0 collective-permute-start.40
  201.7 2.7 %collective-permute-done.41.refs_2_ = f32[16,5,8,128]{3,2,1,0:T(8,128)S(1)} collective-permute-done((f32[16,5,8,128]{3,2,1,0:T(8,128)S(1)}, f32[16,5,8,128]{3,2,1,0:T(8,128)S(1)}, u32[]{:S(2)}, u32[]{:S(2)}) %collective-permute-start.41) | collective-permute-done | bytes 327712 | tf_op jit(solution)/shard_map/ppermute | solution.py:345
  204.4 1.6 collective-permute-start.42
  206.0 2.6 %collective-permute-done.40.refs_8_.refs_1_ = f32[8,5,16,128]{3,2,1,0:T(8,128)S(1)} collective-permute-done((f32[8,5,16,128]{3,2,1,0:T(8,128)S(1)}, f32[8,5,16,128]{3,2,1,0:T(8,128)S(1)}, u32[]{:S(2)}, u32[]{:S(2)}) %collective-permute-start.40) | collective-permute-done | bytes 327712 | tf_op jit(solution)/shard_map/ppermute | solution.py:353
  214.8 1.4 collective-permute-done.46.refs_17_
  216.2 3.1 %place_one.1 = f32[8,5,128,128]{3,2,1,0:T(8,128)} custom-call(s32[1]{0:T(128)} %bitcast.place_ref, f32[8,5,8,128]{3,2,1,0:T(8,128)S(1)} %get-tuple-element.205.refs_0_, f32[8,5,16,128]{3,2,1,0:T(8,128)S(1)} %get-tuple-element.242.refs_0_.refs_1_, f32[8,5,16,128]{3,2,1,0:T(8,128)S(1)} %get-tuple-element.268.refs_0_.refs_2_, ...), custom_call_target="tpu_custom_call" | custom-call | bytes 5242880 | tf_op jit(solution)/shard_map/place_one/pallas_call | solution.py:214
  219.3 13.9 %collective-permute-done.47.refs_18_ = f32[4,5,16,128]{3,2,1,0:T(8,128)S(1)} collective-permute-done((f32[4,5,16,128]{3,2,1,0:T(8,128)S(1)}, f32[4,5,16,128]{3,2,1,0:T(8,128)S(1)}, u32[]{:S(2)}, u32[]{:S(2)}) %collective-permute-start.47) | collective-permute-done | bytes 163872 | tf_op jit(solution)/shard_map/ppermute | solution.py:459
  233.6 2.6 %last.1 = f32[4,5,128,128]{3,2,1,0:T(8,128)} custom-call(s32[1]{0:T(128)} %bitcast.place_ref, f32[128,128]{1,0:T(8,128)S(1)} %copy-done.2, f32[4,5,16,128]{3,2,1,0:T(8,128)S(1)} %get-tuple-element.298.refs_0_, f32[4,5,16,128]{3,2,1,0:T(8,128)S(1)} %collective-permute-done.13.refs_1_, f32[4,5,16,128]{3,2,1,0:T(8,128)S(1)} %collective-permute-done.14.refs_2_, ...), custom_call_target="tpu_custom_call" | custom-call | flops 671088640 | bytes 6553600 | tf_op jit(solution)/shard_map/last/pallas_call | solution.py:261
  (128 shorter events, 35.6 us)
Async XLA Ops:
  0.6 10.8 %collective-permute-start.1 = (f32[16,128]{1,0:T(8,128)}, f32[16,128]{1,0:T(8,128)S(1)}, u32[]{:S(2)}, u32[]{:S(2)}) collective-permute-start(f32[16,128]{1,0:T(8,128)} %param.21), channel_id=1, source_target_pairs={{0,1},{1,2},{2,3},{3,4},{4,5},{5,6},{6,7},{7,8},{8,9},{9,10},{10,1... | collective-permute-start | bytes 24584 | tf_op jit(solution)/shard_map/ppermute | solution.py:292
  3.6 7.8 %collective-permute-start.2 = (f32[16,128]{1,0:T(8,128)}, f32[16,128]{1,0:T(8,128)S(1)}, u32[]{:S(2)}, u32[]{:S(2)}) collective-permute-start(f32[16,128]{1,0:T(8,128)} %param.21), channel_id=1, source_target_pairs={{0,31},{1,0},{2,1},{3,2},{4,3},{5,4},{6,5},{7,6},{8,7},{9,8},{10,9... | collective-permute-start | bytes 24584 | tf_op jit(solution)/shard_map/ppermute | solution.py:293
  25.6 8.2 %collective-permute-start.4 = (f32[16,5,8,128]{3,2,1,0:T(8,128)S(1)}, f32[16,5,8,128]{3,2,1,0:T(8,128)S(1)}, u32[]{:S(2)}, u32[]{:S(2)}) collective-permute-start(f32[16,5,8,128]{3,2,1,0:T(8,128)S(1)} %get-tuple-element.166), channel_id=1, source_target_pairs={{0,1},{1,0},{2,3},{3,2},{4,5},{5,4},{6,7},{7,6},{8,9},{9,8},{10,11... | collective-permute-start | bytes 983048 | tf_op jit(solution)/shard_map/ppermute | solution.py:353
  25.6 14.7 %collective-permute-start.5 = (f32[16,5,8,128]{3,2,1,0:T(8,128)S(1)}, f32[16,5,8,128]{3,2,1,0:T(8,128)S(1)}, u32[]{:S(2)}, u32[]{:S(2)}) collective-permute-start(f32[16,5,8,128]{3,2,1,0:T(8,128)S(1)} %get-tuple-element.169.refs_0_), channel_id=1, source_target_pairs={{0,2},{1,3},{6,4},{7,5},{8,10},{9,11},{14,12},{15,13},{16,18},{17,... | collective-permute-start | bytes 983048 | tf_op jit(solution)/shard_map/ppermute | solution.py:345
  33.8 11.8 %collective-permute-start.6 = (f32[16,5,8,128]{3,2,1,0:T(8,128)S(1)}, f32[16,5,8,128]{3,2,1,0:T(8,128)S(1)}, u32[]{:S(2)}, u32[]{:S(2)}) collective-permute-start(f32[16,5,8,128]{3,2,1,0:T(8,128)S(1)} %collective-permute-done.4.refs_1_), channel_id=1, source_target_pairs={{0,2},{1,3},{6,4},{7,5},{8,10},{9,11},{14,12},{15,13},{16,18},{17,... | collective-permute-start | bytes 983048 | tf_op jit(solution)/shard_map/ppermute | solution.py:345
  35.1 5.2 %collective-permute-start.3 = (s32[2,16]{1,0:T(2,128)S(1)}, s32[2,16]{1,0:T(2,128)S(1)}, u32[]{:S(2)}, u32[]{:S(2)}) collective-permute-start(s32[2,16]{1,0:T(2,128)S(1)} %pad_add_fusion.1), channel_id=1, source_target_pairs={{0,2},{1,3},{6,4},{7,5},{8,10},{9,11},{14,12},{15,13},{16,18},{17,... | collective-permute-start | bytes 392 | tf_op jit(solution)/shard_map/ppermute | solution.py:345
  36.4 15.3 %collective-permute-start.9 = (f32[16,5,16,128]{3,2,1,0:T(8,128)}, f32[16,5,16,128]{3,2,1,0:T(8,128)}, u32[]{:S(2)}, u32[]{:S(2)}) collective-permute-start(f32[16,5,16,128]{3,2,1,0:T(8,128)} %get-tuple-element.182), channel_id=1, source_target_pairs={{0,1},{1,0},{2,3},{3,2},{4,5},{5,4},{6,7},{7,6},{8,9},{9,8},{10,11... | collective-permute-start | bytes 1966088 | tf_op jit(solution)/shard_map/ppermute | solution.py:353
  40.3 18.0 %collective-permute-start.10 = (f32[16,5,16,128]{3,2,1,0:T(8,128)}, f32[16,5,16,128]{3,2,1,0:T(8,128)}, u32[]{:S(2)}, u32[]{:S(2)}) collective-permute-start(f32[16,5,16,128]{3,2,1,0:T(8,128)} %get-tuple-element.193.refs_0_), channel_id=1, source_target_pairs={{0,2},{1,3},{6,4},{7,5},{8,10},{9,11},{14,12},{15,13},{16,18},{17,... | collective-permute-start | bytes 1966088 | tf_op jit(solution)/shard_map/ppermute | solution.py:345
  49.2 9.1 %collective-permute-start.7 = (f32[32,5,8,128]{3,2,1,0:T(8,128)}, f32[32,5,8,128]{3,2,1,0:T(8,128)S(1)}, u32[]{:S(2)}, u32[]{:S(2)}) collective-permute-start(f32[32,5,8,128]{3,2,1,0:T(8,128)} %get-tuple-element.174), channel_id=1, source_target_pairs={{2,4},{3,5},{4,2},{5,3},{10,12},{11,13},{12,10},{13,11},{18,20},{1... | collective-permute-start | bytes 1966088 | tf_op jit(solution)/shard_map/ppermute | solution.py:421
  50.1 35.8 %collective-permute-start.17 = (f32[16,5,16,128]{3,2,1,0:T(8,128)}, f32[16,5,16,128]{3,2,1,0:T(8,128)}, u32[]{:S(2)}, u32[]{:S(2)}) collective-permute-start(f32[16,5,16,128]{3,2,1,0:T(8,128)} %copy-done.7), channel_id=1, source_target_pairs={{0,1},{1,0},{2,3},{3,2},{4,5},{5,4},{6,7},{7,6},{8,9},{9,8},{10,11... | collective-permute-start | bytes 1966088 | tf_op jit(solution)/shard_map/ppermute | solution.py:353
  51.8 19.7 %collective-permute-start.11 = (f32[16,5,16,128]{3,2,1,0:T(8,128)}, f32[16,5,16,128]{3,2,1,0:T(8,128)}, u32[]{:S(2)}, u32[]{:S(2)}) collective-permute-start(f32[16,5,16,128]{3,2,1,0:T(8,128)} %collective-permute-done.9.refs_1_), channel_id=1, source_target_pairs={{0,2},{1,3},{6,4},{7,5},{8,10},{9,11},{14,12},{15,13},{16,18},{17,... | collective-permute-start | bytes 1966088 | tf_op jit(solution)/shard_map/ppermute | solution.py:345
  73.8 43.2 %collective-permute-start.16 = (f32[32,5,16,128]{3,2,1,0:T(8,128)S(1)}, f32[32,5,16,128]{3,2,1,0:T(8,128)S(1)}, u32[]{:S(2)}, u32[]{:S(2)}) collective-permute-start(f32[32,5,16,128]{3,2,1,0:T(8,128)S(1)} %get-tuple-element.197), channel_id=1, source_target_pairs={{2,4},{3,5},{4,2},{5,3},{10,12},{11,13},{12,10},{13,11},{18,20},{1... | collective-permute-start | bytes 3932168 | tf_op jit(solution)/shard_map/ppermute | solution.py:421
  74.6 26.4 %collective-permute-start.18 = (f32[16,5,16,128]{3,2,1,0:T(8,128)S(1)}, f32[16,5,16,128]{3,2,1,0:T(8,128)S(1)}, u32[]{:S(2)}, u32[]{:S(2)}) collective-permute-start(f32[16,5,16,128]{3,2,1,0:T(8,128)S(1)} %copy-done.6), channel_id=1, source_target_pairs={{0,2},{1,3},{6,4},{7,5},{8,10},{9,11},{14,12},{15,13},{16,18},{17,... | collective-permute-start | bytes 1966088 | tf_op jit(solution)/shard_map/ppermute | solution.py:345
  85.9 29.3 %collective-permute-start.19 = (f32[16,5,16,128]{3,2,1,0:T(8,128)}, f32[16,5,16,128]{3,2,1,0:T(8,128)S(1)}, u32[]{:S(2)}, u32[]{:S(2)}) collective-permute-start(f32[16,5,16,128]{3,2,1,0:T(8,128)} %collective-permute-done.17.refs_1_), channel_id=1, source_target_pairs={{0,2},{1,3},{6,4},{7,5},{8,10},{9,11},{14,12},{15,13},{16,18},{17,... | collective-permute-start | bytes 1966088 | tf_op jit(solution)/shard_map/ppermute | solution.py:345
  87.2 9.3 %collective-permute-start.8 = (f32[16,5,8,128]{3,2,1,0:T(8,128)S(1)}, f32[16,5,8,128]{3,2,1,0:T(8,128)S(1)}, u32[]{:S(2)}, u32[]{:S(2)}) collective-permute-start(f32[16,5,8,128]{3,2,1,0:T(8,128)S(1)} %copy-done.11), channel_id=1, source_target_pairs={{2,0},{3,1},{4,6},{5,7},{10,8},{11,9},{12,14},{13,15},{18,16},{19,... | collective-permute-start | bytes 983048 | tf_op jit(solution)/shard_map/ppermute | solution.py:345
  88.6 29.9 %collective-permute-start.22 = (f32[16,5,16,128]{3,2,1,0:T(8,128)S(1)}, f32[16,5,16,128]{3,2,1,0:T(8,128)S(1)}, u32[]{:S(2)}, u32[]{:S(2)}) collective-permute-start(f32[16,5,16,128]{3,2,1,0:T(8,128)S(1)} %copy-done.4), channel_id=1, source_target_pairs={{0,1},{1,0},{2,3},{3,2},{4,5},{5,4},{6,7},{7,6},{8,9},{9,8},{10,11... | collective-permute-start | bytes 1966088 | tf_op jit(solution)/shard_map/ppermute | solution.py:353
  96.6 10.9 %collective-permute-start.12 = (f32[8,5,8,128]{3,2,1,0:T(8,128)S(1)}, f32[8,5,8,128]{3,2,1,0:T(8,128)S(1)}, u32[]{:S(2)}, u32[]{:S(2)}) collective-permute-start(f32[8,5,8,128]{3,2,1,0:T(8,128)S(1)} %get-tuple-element.202), channel_id=1, source_target_pairs={{0,1},{1,0},{2,3},{3,2},{4,5},{5,4},{6,7},{7,6},{8,9},{9,8},{10,11... | collective-permute-start | bytes 491528 | tf_op jit(solution)/shard_map/ppermute | solution.py:353
  101.0 28.1 %collective-permute-start.23 = (f32[16,5,16,128]{3,2,1,0:T(8,128)S(1)}, f32[16,5,16,128]{3,2,1,0:T(8,128)S(1)}, u32[]{:S(2)}, u32[]{:S(2)}) collective-permute-start(f32[16,5,16,128]{3,2,1,0:T(8,128)S(1)} %get-tuple-element.237.refs_0_), channel_id=1, source_target_pairs={{0,2},{1,3},{6,4},{7,5},{8,10},{9,11},{14,12},{15,13},{16,18},{17,... | collective-permute-start | bytes 1966088 | tf_op jit(solution)/shard_map/ppermute | solution.py:345
  117.1 12.7 %collective-permute-start.20 = (f32[16,5,16,128]{3,2,1,0:T(8,128)S(1)}, f32[16,5,16,128]{3,2,1,0:T(8,128)S(1)}, u32[]{:S(2)}, u32[]{:S(2)}) collective-permute-start(f32[16,5,16,128]{3,2,1,0:T(8,128)S(1)} %get-tuple-element.225), channel_id=1, source_target_pairs={{2,0},{3,1},{4,6},{5,7},{10,8},{11,9},{12,14},{13,15},{18,16},{19,... | collective-permute-start | bytes 1966088 | tf_op jit(solution)/shard_map/ppermute | solution.py:345
  118.4 21.8 %collective-permute-start.24 = (f32[16,5,16,128]{3,2,1,0:T(8,128)S(1)}, f32[16,5,16,128]{3,2,1,0:T(8,128)S(1)}, u32[]{:S(2)}, u32[]{:S(2)}) collective-permute-start(f32[16,5,16,128]{3,2,1,0:T(8,128)S(1)} %collective-permute-done.22.refs_1_), channel_id=1, source_target_pairs={{0,2},{1,3},{6,4},{7,5},{8,10},{9,11},{14,12},{15,13},{16,18},{17,... | collective-permute-start | bytes 1966088 | tf_op jit(solution)/shard_map/ppermute | solution.py:345
  123.1 29.9 %collective-permute-start.28 = (f32[32,5,16,128]{3,2,1,0:T(8,128)S(1)}, f32[32,5,16,128]{3,2,1,0:T(8,128)S(1)}, u32[]{:S(2)}, u32[]{:S(2)}) collective-permute-start(f32[32,5,16,128]{3,2,1,0:T(8,128)S(1)} %get-tuple-element.220), channel_id=1, source_target_pairs={{2,4},{3,5},{4,2},{5,3},{10,12},{11,13},{12,10},{13,11},{18,20},{1... | collective-permute-start | bytes 3932168 | tf_op jit(solution)/shard_map/ppermute | solution.py:421
  123.8 16.4 %collective-permute-start.30 = (f32[16,5,8,128]{3,2,1,0:T(8,128)S(1)}, f32[16,5,8,128]{3,2,1,0:T(8,128)S(1)}, u32[]{:S(2)}, u32[]{:S(2)}) collective-permute-start(f32[16,5,8,128]{3,2,1,0:T(8,128)S(1)} %copy-done.9), channel_id=1, source_target_pairs={{0,1},{1,0},{2,3},{3,2},{4,5},{5,4},{6,7},{7,6},{8,9},{9,8},{10,11... | collective-permute-start | bytes 983048 | tf_op jit(solution)/shard_map/ppermute | solution.py:353
  129.1 15.0 %collective-permute-start.13 = (f32[4,5,16,128]{3,2,1,0:T(8,128)S(1)}, f32[4,5,16,128]{3,2,1,0:T(8,128)S(1)}, u32[]{:S(2)}, u32[]{:S(2)}) collective-permute-start(f32[4,5,16,128]{3,2,1,0:T(8,128)S(1)} %get-tuple-element.208), channel_id=1, source_target_pairs={{0,8},{8,16},{16,24},{24,0},{1,9},{9,17},{17,25},{25,1},{2,10},{10... | collective-permute-start | bytes 491528 | tf_op jit(solution)/shard_map/ppermute | solution.py:459
  129.9 15.0 %collective-permute-start.14 = (f32[4,5,16,128]{3,2,1,0:T(8,128)S(1)}, f32[4,5,16,128]{3,2,1,0:T(8,128)S(1)}, u32[]{:S(2)}, u32[]{:S(2)}) collective-permute-start(f32[4,5,16,128]{3,2,1,0:T(8,128)S(1)} %get-tuple-element.209), channel_id=1, source_target_pairs={{0,16},{8,24},{16,0},{24,8},{1,17},{9,25},{17,1},{25,9},{2,18},{10... | collective-permute-start | bytes 491528 | tf_op jit(solution)/shard_map/ppermute | solution.py:459
  140.2 10.5 %collective-permute-start.15 = (f32[4,5,16,128]{3,2,1,0:T(8,128)S(1)}, f32[4,5,16,128]{3,2,1,0:T(8,128)S(1)}, u32[]{:S(2)}, u32[]{:S(2)}) collective-permute-start(f32[4,5,16,128]{3,2,1,0:T(8,128)S(1)} %get-tuple-element.210), channel_id=1, source_target_pairs={{0,24},{8,0},{16,8},{24,16},{1,25},{9,1},{17,9},{25,17},{2,26},{10... | collective-permute-start | bytes 491528 | tf_op jit(solution)/shard_map/ppermute | solution.py:459
  140.2 11.8 %collective-permute-start.21 = (f32[8,5,16,128]{3,2,1,0:T(8,128)S(1)}, f32[8,5,16,128]{3,2,1,0:T(8,128)S(1)}, u32[]{:S(2)}, u32[]{:S(2)}) collective-permute-start(f32[8,5,16,128]{3,2,1,0:T(8,128)S(1)} %get-tuple-element.230), channel_id=1, source_target_pairs={{0,1},{1,0},{2,3},{3,2},{4,5},{5,4},{6,7},{7,6},{8,9},{9,8},{10,11... | collective-permute-start | bytes 983048 | tf_op jit(solution)/shard_map/ppermute | solution.py:353
  144.1 36.7 %collective-permute-start.37 = (f32[32,5,16,128]{3,2,1,0:T(8,128)S(1)}, f32[32,5,16,128]{3,2,1,0:T(8,128)S(1)}, u32[]{:S(2)}, u32[]{:S(2)}) collective-permute-start(f32[32,5,16,128]{3,2,1,0:T(8,128)S(1)} %get-tuple-element.241), channel_id=1, source_target_pairs={{2,4},{3,5},{4,2},{5,3},{10,12},{11,13},{12,10},{13,11},{18,20},{1... | collective-permute-start | bytes 3932168 | tf_op jit(solution)/shard_map/ppermute | solution.py:421
  144.9 13.9 %collective-permute-start.32 = (f32[16,5,8,128]{3,2,1,0:T(8,128)S(1)}, f32[16,5,8,128]{3,2,1,0:T(8,128)S(1)}, u32[]{:S(2)}, u32[]{:S(2)}) collective-permute-start(f32[16,5,8,128]{3,2,1,0:T(8,128)S(1)} %collective-permute-done.30.refs_1_), channel_id=1, source_target_pairs={{0,2},{1,3},{6,4},{7,5},{8,10},{9,11},{14,12},{15,13},{16,18},{17,... | collective-permute-start | bytes 983048 | tf_op jit(solution)/shard_map/ppermute | solution.py:345
  150.7 14.1 %collective-permute-start.31 = (f32[16,5,8,128]{3,2,1,0:T(8,128)S(1)}, f32[16,5,8,128]{3,2,1,0:T(8,128)S(1)}, u32[]{:S(2)}, u32[]{:S(2)}) collective-permute-start(f32[16,5,8,128]{3,2,1,0:T(8,128)S(1)} %get-tuple-element.256.refs_0_), channel_id=1, source_target_pairs={{0,2},{1,3},{6,4},{7,5},{8,10},{9,11},{14,12},{15,13},{16,18},{17,... | collective-permute-start | bytes 983048 | tf_op jit(solution)/shard_map/ppermute | solution.py:345
  153.1 18.2 %collective-permute-start.29 = (f32[16,5,16,128]{3,2,1,0:T(8,128)S(1)}, f32[16,5,16,128]{3,2,1,0:T(8,128)S(1)}, u32[]{:S(2)}, u32[]{:S(2)}) collective-permute-start(f32[16,5,16,128]{3,2,1,0:T(8,128)S(1)} %get-tuple-element.253), channel_id=1, source_target_pairs={{2,0},{3,1},{4,6},{5,7},{10,8},{11,9},{12,14},{13,15},{18,16},{19,... | collective-permute-start | bytes 1966088 | tf_op jit(solution)/shard_map/ppermute | solution.py:345
  154.4 18.2 %collective-permute-start.25 = (f32[4,5,32,128]{3,2,1,0:T(8,128)S(1)}, f32[4,5,32,128]{3,2,1,0:T(8,128)S(1)}, u32[]{:S(2)}, u32[]{:S(2)}) collective-permute-start(f32[4,5,32,128]{3,2,1,0:T(8,128)S(1)} %get-tuple-element.245), channel_id=1, source_target_pairs={{0,8},{8,16},{16,24},{24,0},{1,9},{9,17},{17,25},{25,1},{2,10},{10... | collective-permute-start | bytes 983048 | tf_op jit(solution)/shard_map/ppermute | solution.py:459
  158.7 14.5 %collective-permute-start.26 = (f32[4,5,32,128]{3,2,1,0:T(8,128)S(1)}, f32[4,5,32,128]{3,2,1,0:T(8,128)S(1)}, u32[]{:S(2)}, u32[]{:S(2)}) collective-permute-start(f32[4,5,32,128]{3,2,1,0:T(8,128)S(1)} %get-tuple-element.246), channel_id=1, source_target_pairs={{0,16},{8,24},{16,0},{24,8},{1,17},{9,25},{17,1},{25,9},{2,18},{10... | collective-permute-start | bytes 983048 | tf_op jit(solution)/shard_map/ppermute | solution.py:459
  164.8 8.5 %collective-permute-start.27 = (f32[4,5,32,128]{3,2,1,0:T(8,128)S(1)}, f32[4,5,32,128]{3,2,1,0:T(8,128)S(1)}, u32[]{:S(2)}, u32[]{:S(2)}) collective-permute-start(f32[4,5,32,128]{3,2,1,0:T(8,128)S(1)} %get-tuple-element.247), channel_id=1, source_target_pairs={{0,24},{8,0},{16,8},{24,16},{1,25},{9,1},{17,9},{25,17},{2,26},{10... | collective-permute-start | bytes 983048 | tf_op jit(solution)/shard_map/ppermute | solution.py:459
  171.4 8.5 %collective-permute-start.33 = (f32[8,5,16,128]{3,2,1,0:T(8,128)S(1)}, f32[8,5,16,128]{3,2,1,0:T(8,128)S(1)}, u32[]{:S(2)}, u32[]{:S(2)}) collective-permute-start(f32[8,5,16,128]{3,2,1,0:T(8,128)S(1)} %get-tuple-element.265), channel_id=1, source_target_pairs={{0,1},{1,0},{2,3},{3,2},{4,5},{5,4},{6,7},{7,6},{8,9},{9,8},{10,11... | collective-permute-start | bytes 983048 | tf_op jit(solution)/shard_map/ppermute | solution.py:353
  172.6 9.7 %collective-permute-start.39 = (f32[32,5,8,128]{3,2,1,0:T(8,128)S(1)}, f32[32,5,8,128]{3,2,1,0:T(8,128)S(1)}, u32[]{:S(2)}, u32[]{:S(2)}) collective-permute-start(f32[32,5,8,128]{3,2,1,0:T(8,128)S(1)} %get-tuple-element.260), channel_id=1, source_target_pairs={{2,4},{3,5},{4,2},{5,3},{10,12},{11,13},{12,10},{13,11},{18,20},{1... | collective-permute-start | bytes 1966088 | tf_op jit(solution)/shard_map/ppermute | solution.py:421
  180.9 18.7 %collective-permute-start.38 = (f32[16,5,16,128]{3,2,1,0:T(8,128)S(1)}, f32[16,5,16,128]{3,2,1,0:T(8,128)S(1)}, u32[]{:S(2)}, u32[]{:S(2)}) collective-permute-start(f32[16,5,16,128]{3,2,1,0:T(8,128)S(1)} %get-tuple-element.279), channel_id=1, source_target_pairs={{2,0},{3,1},{4,6},{5,7},{10,8},{11,9},{12,14},{13,15},{18,16},{19,... | collective-permute-start | bytes 1966088 | tf_op jit(solution)/shard_map/ppermute | solution.py:345
  182.3 22.0 %collective-permute-start.41 = (f32[16,5,8,128]{3,2,1,0:T(8,128)S(1)}, f32[16,5,8,128]{3,2,1,0:T(8,128)S(1)}, u32[]{:S(2)}, u32[]{:S(2)}) collective-permute-start(f32[16,5,8,128]{3,2,1,0:T(8,128)S(1)} %get-tuple-element.283), channel_id=1, source_target_pairs={{2,0},{3,1},{4,6},{5,7},{10,8},{11,9},{12,14},{13,15},{18,16},{19,... | collective-permute-start | bytes 983048 | tf_op jit(solution)/shard_map/ppermute | solution.py:345
  183.6 22.3 %collective-permute-start.34 = (f32[4,5,32,128]{3,2,1,0:T(8,128)S(1)}, f32[4,5,32,128]{3,2,1,0:T(8,128)S(1)}, u32[]{:S(2)}, u32[]{:S(2)}) collective-permute-start(f32[4,5,32,128]{3,2,1,0:T(8,128)S(1)} %get-tuple-element.271), channel_id=1, source_target_pairs={{0,8},{8,16},{16,24},{24,0},{1,9},{9,17},{17,25},{25,1},{2,10},{10... | collective-permute-start | bytes 983048 | tf_op jit(solution)/shard_map/ppermute | solution.py:459
  183.7 22.3 %collective-permute-start.35 = (f32[4,5,32,128]{3,2,1,0:T(8,128)S(1)}, f32[4,5,32,128]{3,2,1,0:T(8,128)S(1)}, u32[]{:S(2)}, u32[]{:S(2)}) collective-permute-start(f32[4,5,32,128]{3,2,1,0:T(8,128)S(1)} %get-tuple-element.272), channel_id=1, source_target_pairs={{0,16},{8,24},{16,0},{24,8},{1,17},{9,25},{17,1},{25,9},{2,18},{10... | collective-permute-start | bytes 983048 | tf_op jit(solution)/shard_map/ppermute | solution.py:459
  183.8 22.2 %collective-permute-start.36 = (f32[4,5,32,128]{3,2,1,0:T(8,128)S(1)}, f32[4,5,32,128]{3,2,1,0:T(8,128)S(1)}, u32[]{:S(2)}, u32[]{:S(2)}) collective-permute-start(f32[4,5,32,128]{3,2,1,0:T(8,128)S(1)} %get-tuple-element.273), channel_id=1, source_target_pairs={{0,24},{8,0},{16,8},{24,16},{1,25},{9,1},{17,9},{25,17},{2,26},{10... | collective-permute-start | bytes 983048 | tf_op jit(solution)/shard_map/ppermute | solution.py:459
  199.7 8.9 %collective-permute-start.40 = (f32[8,5,16,128]{3,2,1,0:T(8,128)S(1)}, f32[8,5,16,128]{3,2,1,0:T(8,128)S(1)}, u32[]{:S(2)}, u32[]{:S(2)}) collective-permute-start(f32[8,5,16,128]{3,2,1,0:T(8,128)S(1)} %get-tuple-element.288), channel_id=1, source_target_pairs={{0,1},{1,0},{2,3},{3,2},{4,5},{5,4},{6,7},{7,6},{8,9},{9,8},{10,11... | collective-permute-start | bytes 983048 | tf_op jit(solution)/shard_map/ppermute | solution.py:353
  204.4 5.9 %collective-permute-start.42 = (f32[8,5,8,128]{3,2,1,0:T(8,128)S(1)}, f32[8,5,8,128]{3,2,1,0:T(8,128)S(1)}, u32[]{:S(2)}, u32[]{:S(2)}) collective-permute-start(f32[8,5,8,128]{3,2,1,0:T(8,128)S(1)} %get-tuple-element.297), channel_id=1, source_target_pairs={{0,1},{1,0},{2,3},{3,2},{4,5},{5,4},{6,7},{7,6},{8,9},{9,8},{10,11... | collective-permute-start | bytes 491528 | tf_op jit(solution)/shard_map/ppermute | solution.py:353
  211.2 5.0 %collective-permute-start.46 = (f32[4,5,16,128]{3,2,1,0:T(8,128)S(1)}, f32[4,5,16,128]{3,2,1,0:T(8,128)S(1)}, u32[]{:S(2)}, u32[]{:S(2)}) collective-permute-start(f32[4,5,16,128]{3,2,1,0:T(8,128)S(1)} %get-tuple-element.319), channel_id=1, source_target_pairs={{0,8},{8,16},{16,24},{24,0},{1,9},{9,17},{17,25},{25,1},{2,10},{10... | collective-permute-start | bytes 491528 | tf_op jit(solution)/shard_map/ppermute | solution.py:459
  211.2 22.3 %collective-permute-start.43 = (f32[4,5,32,128]{3,2,1,0:T(8,128)S(1)}, f32[4,5,32,128]{3,2,1,0:T(8,128)S(1)}, u32[]{:S(2)}, u32[]{:S(2)}) collective-permute-start(f32[4,5,32,128]{3,2,1,0:T(8,128)S(1)} %get-tuple-element.313), channel_id=1, source_target_pairs={{0,8},{8,16},{16,24},{24,0},{1,9},{9,17},{17,25},{25,1},{2,10},{10... | collective-permute-start | bytes 983048 | tf_op jit(solution)/shard_map/ppermute | solution.py:459
  212.1 21.5 %collective-permute-start.44 = (f32[4,5,32,128]{3,2,1,0:T(8,128)S(1)}, f32[4,5,32,128]{3,2,1,0:T(8,128)S(1)}, u32[]{:S(2)}, u32[]{:S(2)}) collective-permute-start(f32[4,5,32,128]{3,2,1,0:T(8,128)S(1)} %get-tuple-element.314), channel_id=1, source_target_pairs={{0,16},{8,24},{16,0},{24,8},{1,17},{9,25},{17,1},{25,9},{2,18},{10... | collective-permute-start | bytes 983048 | tf_op jit(solution)/shard_map/ppermute | solution.py:459
  213.4 20.2 %collective-permute-start.45 = (f32[4,5,32,128]{3,2,1,0:T(8,128)S(1)}, f32[4,5,32,128]{3,2,1,0:T(8,128)S(1)}, u32[]{:S(2)}, u32[]{:S(2)}) collective-permute-start(f32[4,5,32,128]{3,2,1,0:T(8,128)S(1)} %get-tuple-element.315), channel_id=1, source_target_pairs={{0,24},{8,0},{16,8},{24,16},{1,25},{9,1},{17,9},{25,17},{2,26},{10... | collective-permute-start | bytes 983048 | tf_op jit(solution)/shard_map/ppermute | solution.py:459
  213.5 19.8 %collective-permute-start.47 = (f32[4,5,16,128]{3,2,1,0:T(8,128)S(1)}, f32[4,5,16,128]{3,2,1,0:T(8,128)S(1)}, u32[]{:S(2)}, u32[]{:S(2)}) collective-permute-start(f32[4,5,16,128]{3,2,1,0:T(8,128)S(1)} %get-tuple-element.320), channel_id=1, source_target_pairs={{0,16},{8,24},{16,0},{24,8},{1,17},{9,25},{17,1},{25,9},{2,18},{10... | collective-permute-start | bytes 491528 | tf_op jit(solution)/shard_map/ppermute | solution.py:459
  216.2 17.3 %collective-permute-start.48 = (f32[4,5,16,128]{3,2,1,0:T(8,128)S(1)}, f32[4,5,16,128]{3,2,1,0:T(8,128)S(1)}, u32[]{:S(2)}, u32[]{:S(2)}) collective-permute-start(f32[4,5,16,128]{3,2,1,0:T(8,128)S(1)} %get-tuple-element.321), channel_id=1, source_target_pairs={{0,24},{8,0},{16,8},{24,16},{1,25},{9,1},{17,9},{25,17},{2,26},{10... | collective-permute-start | bytes 491528 | tf_op jit(solution)/shard_map/ppermute | solution.py:459
  (21 other events, 194.3 us)
